TPU v7x, 256 devices: a whole 4x4x8 slice. The times are simulated.
256 devices in a mesh: ctx: 32 (over z, y), head: 8 (over x, core).
Axes of the slice: x: 4, y: 4, z: 8, core: 2. Of those that a mesh axis runs over, the one named last changes fastest.
Arguments:
- queries: bfloat16 [16384, 8192], P('ctx', 'head'), may hold values from -6 to 6
- keys: bfloat16 [16384, 1024], P('ctx', 'head'), may hold values from -5 to 5
- values: bfloat16 [16384, 1024], P('ctx', 'head'), may hold values from -6 to 6
- kept: int32 [8, 32, 64], P('head', 'ctx'), may hold values from 0 to 511, all different within a row
Outputs:
- attended: bfloat16 [16384, 8192], P('ctx', 'head')
Inputs may be any that keep to these rules, and one draw needn't show every extreme that they name: Each row kept[h, c] names 64 distinct positions of host c's block.
All inputs are finite; a program needn't handle non-finite values.
Results may differ from a plain program's by a relative error of at most 0.0059.
Values may be sent and summed in bfloat16 or wider, within the bound.
A program may use at most 64 MiB of HBM per device.

v0:
```python
import jax
import jax.numpy as jnp
from jax import lax
from jax.sharding import PartitionSpec as P

HEAD_DIM = 128
QUERY_PER_KV = 8
ANCHOR_TOKENS = 256


NEG = -1e30


def broadcast(x, axis, root):
    mine = lax.axis_index(axis) == root
    return lax.psum(jnp.where(mine, x, jnp.zeros_like(x)), axis)


def for_sending(x):

    def short(part):
        return part.astype(jnp.bfloat16) if part.dtype == jnp.float32 else part

    return jax.tree.map(short, x)


def from_behind(block, axis, distance):
    devices = range(lax.axis_size(axis))
    route = [(i - distance, i) for i in devices if i - distance in devices]
    return lax.ppermute(block, axis, route)


def fold_head(acc, top, total, qrows, khead, vhead, valid, key_tok):
    row_items = qrows.shape[0]
    width = min(row_items, 512)
    count = row_items // width
    scale = HEAD_DIM ** (-0.5)

    def block(args):
        qblock, ablock, mblock, tblock, index = args
        scores = jnp.dot(qblock, khead.T, preferred_element_type=jnp.float32) * scale
        mask = jnp.broadcast_to(valid[None, :], scores.shape)
        if key_tok is not None:
            row_tok = (index * width + jnp.arange(width, dtype=jnp.int32)) // QUERY_PER_KV
            mask = mask & (key_tok[None, :] <= row_tok[:, None])
        newtop = jnp.maximum(mblock, jnp.max(jnp.where(mask, scores, NEG), axis=1))
        weight = jnp.where(mask, jnp.exp(scores - newtop[:, None]), 0.0)
        factor = jnp.exp(mblock - newtop)
        newtotal = tblock * factor + jnp.sum(weight, axis=1)
        newacc = ablock * factor[:, None] + jnp.dot(
            weight.astype(jnp.bfloat16), vhead, preferred_element_type=jnp.float32
        )
        return (newacc, newtop, newtotal)

    outs = lax.map(
        block,
        (
            qrows.reshape(count, width, -1),
            acc.reshape(count, width, -1),
            top.reshape(count, width),
            total.reshape(count, width),
            jnp.arange(count, dtype=jnp.int32),
        ),
    )
    return (outs[0].reshape(row_items, -1), outs[1].reshape(row_items), outs[2].reshape(row_items))


def fold(states, qheads, key_rows, value_rows, valid, key_tok):
    acc, top, total = states
    accs, tops, totals = ([], [], [])
    final_output = fold_head(
        acc[0], top[0], total[0], qheads[0], key_rows, value_rows, valid, key_tok
    )
    accs.append(final_output[0])
    tops.append(final_output[1])
    totals.append(final_output[2])
    return (jnp.stack(accs), jnp.stack(tops), jnp.stack(totals))


def fold_when(states, flag, qheads, key_rows, value_rows, valid):
    return lax.cond(
        flag, lambda st: fold(st, qheads, key_rows, value_rows, valid, None), lambda st: st, states
    )


def empty_states(head_list, row_items):
    return (
        jnp.zeros((head_list, row_items, HEAD_DIM), jnp.float32),
        jnp.full((head_list, row_items), NEG, jnp.float32),
        jnp.zeros((head_list, row_items), jnp.float32),
    )


def as_rows(block_queries, head_list):
    blk = block_queries.shape[0]
    return (
        block_queries.reshape(blk, head_list, QUERY_PER_KV, HEAD_DIM)
        .transpose(1, 0, 2, 3)
        .reshape(head_list, blk * QUERY_PER_KV, HEAD_DIM)
    )


def on_device(queries, keys, values, kept):
    blk = queries.shape[0]
    head_list = keys.shape[1] // HEAD_DIM
    ret = kept.shape[2]
    row_items = blk * QUERY_PER_KV
    hosts = lax.axis_size("ctx")
    me = lax.axis_index("ctx")
    spots = lax.broadcasted_iota(jnp.int32, (ret, blk), 1)
    comp_k, comp_v = ([], [])
    onehot = (kept[0, 0][:, None] == spots).astype(jnp.bfloat16)
    comp_k.append(jnp.dot(onehot, keys, preferred_element_type=jnp.float32).astype(jnp.bfloat16))
    comp_v.append(jnp.dot(onehot, values, preferred_element_type=jnp.float32).astype(jnp.bfloat16))
    compact_keys = comp_k[0]
    compact_values = comp_v[0]
    qheads = as_rows(queries, head_list)
    states = empty_states(head_list, row_items)
    anchor_key_rows, anchor_value_rows = (
        broadcast(keys[:ANCHOR_TOKENS], "ctx", 0),
        broadcast(values[:ANCHOR_TOKENS], "ctx", 0),
    )
    anchor_valid = jnp.broadcast_to(me > 0, (ANCHOR_TOKENS,))
    states = fold(states, qheads, anchor_key_rows, anchor_value_rows, anchor_valid, None)
    kblock = min(blk, 512)
    key_tok = 0 + jnp.arange(kblock, dtype=jnp.int32)
    own_valid = jnp.ones((kblock,), dtype=bool)
    states = fold(states, qheads, keys, values, own_valid, key_tok)
    all_valid = jnp.ones((ret,), dtype=bool)

    def step(index, carry):
        current, piece = carry
        piece = jax.tree.map(
            lambda part, own: part.astype(own.dtype),
            from_behind(for_sending(piece), "ctx", 1),
            piece,
        )
        current = fold_when(current, me > index, qheads, piece[0], piece[1], all_valid)
        return (current, piece)

    states, _ = lax.fori_loop(0, hosts - 1, step, (states, (compact_keys, compact_values)))
    acc, top, total = states
    final_output = acc / total[..., None]
    return (
        final_output.reshape(head_list, blk, QUERY_PER_KV, HEAD_DIM)
        .transpose(1, 0, 2, 3)
        .reshape(blk, head_list * QUERY_PER_KV * HEAD_DIM)
        .astype(jnp.bfloat16)
    )


def solution(mesh):
    placed = (P("ctx", "head"), P("ctx", "head"), P("ctx", "head"), P("head", "ctx", None))
    return jax.shard_map(
        on_device, mesh=mesh, in_specs=placed, out_specs=P("ctx", "head"), check_vma=False
    )
```

profile of v0, /device:TPU:226, one launch (start us, length us, event | category | flops | bytes accessed | tf_op | source)
XLA Modules:
  0.0 1005.2 jit_solution(10985280590149265933)
XLA Ops:
  10.7 139.5 %all-reduce.3.cloned.1.call-done = (bf16[256,128]{1,0:T(8,128)(2,1)}, bf16[256,128]{1,0:T(8,128)(2,1)}) async-done(((bf16[256,128]{1,0:T(8,128)(2,1)}, bf16[256,128]{1,0:T(8,128)(2,1)}), (bf16[256,128]{1,0:T(8,128)(2,1)}, bf16[256,128]{1,0:T(8,128)(2,1)})) %all-reduce.3.cloned.1.call-update) | async-done | bytes 131088 | tf_op jit(solution)/shard_map/psum | solution.py:16
  165.3 34.0 %while.69 = (s32[]{:T(128)}, f32[8,512,128]{2,1,0:T(8,128)S(1)}, f32[8,512]{1,0:T(8,128)S(1)}, f32[8,512]{1,0:T(8,128)S(1)}, f32[8,512,128]{2,1,0:T(8,128)}, /*i...) while((s32[]{:T(128)}, f32[8,512,128]{2,1,0:T(8,128)S(1)}, ...), condition=%wide.region_9.10_spmd.clone, body=%wide.region_6.9_spmd.clone.sunk | while | flops 137504768 | bytes 4115125 | solution.py:55
  199.4 797.0 %while.67 = (s32[]{:T(128)}, f32[1,4096,128]{2,1,0:T(8,128)S(1)}, f32[1,4096]{1,0:T(1,128)S(1)}, f32[1,4096]{1,0:T(1,128)S(1)}, bf16[64,128]{1,0:T(8,128)(2,1)},...) while((s32[]{:T(128)}, f32[1,4096,128]{2,1,0:T(8,128)S(1)}, ...), condition=%wide.region_17.18_spmd, body=%wide.region_10.17_spmd.sunk | while | flops 17106948 | bytes 7810084 | solution.py:141
  210.6 16.2 %conditional.2 = ((f32[1,4096,128]{2,1,0:T(8,128)S(1)}, f32[1,4096]{1,0:T(1,128)S(1)}, f32[1,4096]{1,0:T(1,128)S(1)})) conditional(s32[]{:T(128)} %convert_element_type.51, (f32[1,4096,128]{2,1,0:T(8,128)S(1)}, f32[1,4096]{1,0:T(1,128)S(1)}, f32[1,4096]{1,0:T(1,128)S(1)}) %tuple.103, (bf16[512,1024]{1,0:T(8,128)(2,1)}, ...), branch_computations={%region_11.11_spmd, %region_12.16_spmd} | conditional | flops 17106944 | bytes 7613217 | solution.py:81
  237.0 16.2 %conditional.2 = ((f32[1,4096,128]{2,1,0:T(8,128)S(1)}, f32[1,4096]{1,0:T(1,128)S(1)}, f32[1,4096]{1,0:T(1,128)S(1)})) conditional(s32[]{:T(128)} %convert_element_type.51, (f32[1,4096,128]{2,1,0:T(8,128)S(1)}, f32[1,4096]{1,0:T(1,128)S(1)}, f32[1,4096]{1,0:T(1,128)S(1)}) %tuple.103, (bf16[512,1024]{1,0:T(8,128)(2,1)}, ...), branch_computations={%region_11.11_spmd, %region_12.16_spmd} | conditional | flops 17106944 | bytes 7613217 | solution.py:81
  263.5 16.2 %conditional.2 = ((f32[1,4096,128]{2,1,0:T(8,128)S(1)}, f32[1,4096]{1,0:T(1,128)S(1)}, f32[1,4096]{1,0:T(1,128)S(1)})) conditional(s32[]{:T(128)} %convert_element_type.51, (f32[1,4096,128]{2,1,0:T(8,128)S(1)}, f32[1,4096]{1,0:T(1,128)S(1)}, f32[1,4096]{1,0:T(1,128)S(1)}) %tuple.103, (bf16[512,1024]{1,0:T(8,128)(2,1)}, ...), branch_computations={%region_11.11_spmd, %region_12.16_spmd} | conditional | flops 17106944 | bytes 7613217 | solution.py:81
  289.9 16.2 %conditional.2 = ((f32[1,4096,128]{2,1,0:T(8,128)S(1)}, f32[1,4096]{1,0:T(1,128)S(1)}, f32[1,4096]{1,0:T(1,128)S(1)})) conditional(s32[]{:T(128)} %convert_element_type.51, (f32[1,4096,128]{2,1,0:T(8,128)S(1)}, f32[1,4096]{1,0:T(1,128)S(1)}, f32[1,4096]{1,0:T(1,128)S(1)}) %tuple.103, (bf16[512,1024]{1,0:T(8,128)(2,1)}, ...), branch_computations={%region_11.11_spmd, %region_12.16_spmd} | conditional | flops 17106944 | bytes 7613217 | solution.py:81
  316.4 16.2 %conditional.2 = ((f32[1,4096,128]{2,1,0:T(8,128)S(1)}, f32[1,4096]{1,0:T(1,128)S(1)}, f32[1,4096]{1,0:T(1,128)S(1)})) conditional(s32[]{:T(128)} %convert_element_type.51, (f32[1,4096,128]{2,1,0:T(8,128)S(1)}, f32[1,4096]{1,0:T(1,128)S(1)}, f32[1,4096]{1,0:T(1,128)S(1)}) %tuple.103, (bf16[512,1024]{1,0:T(8,128)(2,1)}, ...), branch_computations={%region_11.11_spmd, %region_12.16_spmd} | conditional | flops 17106944 | bytes 7613217 | solution.py:81
  342.9 16.2 %conditional.2 = ((f32[1,4096,128]{2,1,0:T(8,128)S(1)}, f32[1,4096]{1,0:T(1,128)S(1)}, f32[1,4096]{1,0:T(1,128)S(1)})) conditional(s32[]{:T(128)} %convert_element_type.51, (f32[1,4096,128]{2,1,0:T(8,128)S(1)}, f32[1,4096]{1,0:T(1,128)S(1)}, f32[1,4096]{1,0:T(1,128)S(1)}) %tuple.103, (bf16[512,1024]{1,0:T(8,128)(2,1)}, ...), branch_computations={%region_11.11_spmd, %region_12.16_spmd} | conditional | flops 17106944 | bytes 7613217 | solution.py:81
  369.3 16.2 %conditional.2 = ((f32[1,4096,128]{2,1,0:T(8,128)S(1)}, f32[1,4096]{1,0:T(1,128)S(1)}, f32[1,4096]{1,0:T(1,128)S(1)})) conditional(s32[]{:T(128)} %convert_element_type.51, (f32[1,4096,128]{2,1,0:T(8,128)S(1)}, f32[1,4096]{1,0:T(1,128)S(1)}, f32[1,4096]{1,0:T(1,128)S(1)}) %tuple.103, (bf16[512,1024]{1,0:T(8,128)(2,1)}, ...), branch_computations={%region_11.11_spmd, %region_12.16_spmd} | conditional | flops 17106944 | bytes 7613217 | solution.py:81
  395.8 16.2 %conditional.2 = ((f32[1,4096,128]{2,1,0:T(8,128)S(1)}, f32[1,4096]{1,0:T(1,128)S(1)}, f32[1,4096]{1,0:T(1,128)S(1)})) conditional(s32[]{:T(128)} %convert_element_type.51, (f32[1,4096,128]{2,1,0:T(8,128)S(1)}, f32[1,4096]{1,0:T(1,128)S(1)}, f32[1,4096]{1,0:T(1,128)S(1)}) %tuple.103, (bf16[512,1024]{1,0:T(8,128)(2,1)}, ...), branch_computations={%region_11.11_spmd, %region_12.16_spmd} | conditional | flops 17106944 | bytes 7613217 | solution.py:81
  422.2 16.2 %conditional.2 = ((f32[1,4096,128]{2,1,0:T(8,128)S(1)}, f32[1,4096]{1,0:T(1,128)S(1)}, f32[1,4096]{1,0:T(1,128)S(1)})) conditional(s32[]{:T(128)} %convert_element_type.51, (f32[1,4096,128]{2,1,0:T(8,128)S(1)}, f32[1,4096]{1,0:T(1,128)S(1)}, f32[1,4096]{1,0:T(1,128)S(1)}) %tuple.103, (bf16[512,1024]{1,0:T(8,128)(2,1)}, ...), branch_computations={%region_11.11_spmd, %region_12.16_spmd} | conditional | flops 17106944 | bytes 7613217 | solution.py:81
  448.7 16.2 %conditional.2 = ((f32[1,4096,128]{2,1,0:T(8,128)S(1)}, f32[1,4096]{1,0:T(1,128)S(1)}, f32[1,4096]{1,0:T(1,128)S(1)})) conditional(s32[]{:T(128)} %convert_element_type.51, (f32[1,4096,128]{2,1,0:T(8,128)S(1)}, f32[1,4096]{1,0:T(1,128)S(1)}, f32[1,4096]{1,0:T(1,128)S(1)}) %tuple.103, (bf16[512,1024]{1,0:T(8,128)(2,1)}, ...), branch_computations={%region_11.11_spmd, %region_12.16_spmd} | conditional | flops 17106944 | bytes 7613217 | solution.py:81
  475.1 16.2 %conditional.2 = ((f32[1,4096,128]{2,1,0:T(8,128)S(1)}, f32[1,4096]{1,0:T(1,128)S(1)}, f32[1,4096]{1,0:T(1,128)S(1)})) conditional(s32[]{:T(128)} %convert_element_type.51, (f32[1,4096,128]{2,1,0:T(8,128)S(1)}, f32[1,4096]{1,0:T(1,128)S(1)}, f32[1,4096]{1,0:T(1,128)S(1)}) %tuple.103, (bf16[512,1024]{1,0:T(8,128)(2,1)}, ...), branch_computations={%region_11.11_spmd, %region_12.16_spmd} | conditional | flops 17106944 | bytes 7613217 | solution.py:81
  501.6 16.2 %conditional.2 = ((f32[1,4096,128]{2,1,0:T(8,128)S(1)}, f32[1,4096]{1,0:T(1,128)S(1)}, f32[1,4096]{1,0:T(1,128)S(1)})) conditional(s32[]{:T(128)} %convert_element_type.51, (f32[1,4096,128]{2,1,0:T(8,128)S(1)}, f32[1,4096]{1,0:T(1,128)S(1)}, f32[1,4096]{1,0:T(1,128)S(1)}) %tuple.103, (bf16[512,1024]{1,0:T(8,128)(2,1)}, ...), branch_computations={%region_11.11_spmd, %region_12.16_spmd} | conditional | flops 17106944 | bytes 7613217 | solution.py:81
  528.1 16.2 %conditional.2 = ((f32[1,4096,128]{2,1,0:T(8,128)S(1)}, f32[1,4096]{1,0:T(1,128)S(1)}, f32[1,4096]{1,0:T(1,128)S(1)})) conditional(s32[]{:T(128)} %convert_element_type.51, (f32[1,4096,128]{2,1,0:T(8,128)S(1)}, f32[1,4096]{1,0:T(1,128)S(1)}, f32[1,4096]{1,0:T(1,128)S(1)}) %tuple.103, (bf16[512,1024]{1,0:T(8,128)(2,1)}, ...), branch_computations={%region_11.11_spmd, %region_12.16_spmd} | conditional | flops 17106944 | bytes 7613217 | solution.py:81
  554.5 16.2 %conditional.2 = ((f32[1,4096,128]{2,1,0:T(8,128)S(1)}, f32[1,4096]{1,0:T(1,128)S(1)}, f32[1,4096]{1,0:T(1,128)S(1)})) conditional(s32[]{:T(128)} %convert_element_type.51, (f32[1,4096,128]{2,1,0:T(8,128)S(1)}, f32[1,4096]{1,0:T(1,128)S(1)}, f32[1,4096]{1,0:T(1,128)S(1)}) %tuple.103, (bf16[512,1024]{1,0:T(8,128)(2,1)}, ...), branch_computations={%region_11.11_spmd, %region_12.16_spmd} | conditional | flops 17106944 | bytes 7613217 | solution.py:81
  581.0 16.2 %conditional.2 = ((f32[1,4096,128]{2,1,0:T(8,128)S(1)}, f32[1,4096]{1,0:T(1,128)S(1)}, f32[1,4096]{1,0:T(1,128)S(1)})) conditional(s32[]{:T(128)} %convert_element_type.51, (f32[1,4096,128]{2,1,0:T(8,128)S(1)}, f32[1,4096]{1,0:T(1,128)S(1)}, f32[1,4096]{1,0:T(1,128)S(1)}) %tuple.103, (bf16[512,1024]{1,0:T(8,128)(2,1)}, ...), branch_computations={%region_11.11_spmd, %region_12.16_spmd} | conditional | flops 17106944 | bytes 7613217 | solution.py:81
  607.5 16.2 %conditional.2 = ((f32[1,4096,128]{2,1,0:T(8,128)S(1)}, f32[1,4096]{1,0:T(1,128)S(1)}, f32[1,4096]{1,0:T(1,128)S(1)})) conditional(s32[]{:T(128)} %convert_element_type.51, (f32[1,4096,128]{2,1,0:T(8,128)S(1)}, f32[1,4096]{1,0:T(1,128)S(1)}, f32[1,4096]{1,0:T(1,128)S(1)}) %tuple.103, (bf16[512,1024]{1,0:T(8,128)(2,1)}, ...), branch_computations={%region_11.11_spmd, %region_12.16_spmd} | conditional | flops 17106944 | bytes 7613217 | solution.py:81
  634.0 16.2 %conditional.2 = ((f32[1,4096,128]{2,1,0:T(8,128)S(1)}, f32[1,4096]{1,0:T(1,128)S(1)}, f32[1,4096]{1,0:T(1,128)S(1)})) conditional(s32[]{:T(128)} %convert_element_type.51, (f32[1,4096,128]{2,1,0:T(8,128)S(1)}, f32[1,4096]{1,0:T(1,128)S(1)}, f32[1,4096]{1,0:T(1,128)S(1)}) %tuple.103, (bf16[512,1024]{1,0:T(8,128)(2,1)}, ...), branch_computations={%region_11.11_spmd, %region_12.16_spmd} | conditional | flops 17106944 | bytes 7613217 | solution.py:81
  660.4 16.2 %conditional.2 = ((f32[1,4096,128]{2,1,0:T(8,128)S(1)}, f32[1,4096]{1,0:T(1,128)S(1)}, f32[1,4096]{1,0:T(1,128)S(1)})) conditional(s32[]{:T(128)} %convert_element_type.51, (f32[1,4096,128]{2,1,0:T(8,128)S(1)}, f32[1,4096]{1,0:T(1,128)S(1)}, f32[1,4096]{1,0:T(1,128)S(1)}) %tuple.103, (bf16[512,1024]{1,0:T(8,128)(2,1)}, ...), branch_computations={%region_11.11_spmd, %region_12.16_spmd} | conditional | flops 17106944 | bytes 7613217 | solution.py:81
  686.9 16.2 %conditional.2 = ((f32[1,4096,128]{2,1,0:T(8,128)S(1)}, f32[1,4096]{1,0:T(1,128)S(1)}, f32[1,4096]{1,0:T(1,128)S(1)})) conditional(s32[]{:T(128)} %convert_element_type.51, (f32[1,4096,128]{2,1,0:T(8,128)S(1)}, f32[1,4096]{1,0:T(1,128)S(1)}, f32[1,4096]{1,0:T(1,128)S(1)}) %tuple.103, (bf16[512,1024]{1,0:T(8,128)(2,1)}, ...), branch_computations={%region_11.11_spmd, %region_12.16_spmd} | conditional | flops 17106944 | bytes 7613217 | solution.py:81
  713.3 16.2 %conditional.2 = ((f32[1,4096,128]{2,1,0:T(8,128)S(1)}, f32[1,4096]{1,0:T(1,128)S(1)}, f32[1,4096]{1,0:T(1,128)S(1)})) conditional(s32[]{:T(128)} %convert_element_type.51, (f32[1,4096,128]{2,1,0:T(8,128)S(1)}, f32[1,4096]{1,0:T(1,128)S(1)}, f32[1,4096]{1,0:T(1,128)S(1)}) %tuple.103, (bf16[512,1024]{1,0:T(8,128)(2,1)}, ...), branch_computations={%region_11.11_spmd, %region_12.16_spmd} | conditional | flops 17106944 | bytes 7613217 | solution.py:81
  739.8 16.2 %conditional.2 = ((f32[1,4096,128]{2,1,0:T(8,128)S(1)}, f32[1,4096]{1,0:T(1,128)S(1)}, f32[1,4096]{1,0:T(1,128)S(1)})) conditional(s32[]{:T(128)} %convert_element_type.51, (f32[1,4096,128]{2,1,0:T(8,128)S(1)}, f32[1,4096]{1,0:T(1,128)S(1)}, f32[1,4096]{1,0:T(1,128)S(1)}) %tuple.103, (bf16[512,1024]{1,0:T(8,128)(2,1)}, ...), branch_computations={%region_11.11_spmd, %region_12.16_spmd} | conditional | flops 17106944 | bytes 7613217 | solution.py:81
  766.3 16.2 %conditional.2 = ((f32[1,4096,128]{2,1,0:T(8,128)S(1)}, f32[1,4096]{1,0:T(1,128)S(1)}, f32[1,4096]{1,0:T(1,128)S(1)})) conditional(s32[]{:T(128)} %convert_element_type.51, (f32[1,4096,128]{2,1,0:T(8,128)S(1)}, f32[1,4096]{1,0:T(1,128)S(1)}, f32[1,4096]{1,0:T(1,128)S(1)}) %tuple.103, (bf16[512,1024]{1,0:T(8,128)(2,1)}, ...), branch_computations={%region_11.11_spmd, %region_12.16_spmd} | conditional | flops 17106944 | bytes 7613217 | solution.py:81
  792.7 16.2 %conditional.2 = ((f32[1,4096,128]{2,1,0:T(8,128)S(1)}, f32[1,4096]{1,0:T(1,128)S(1)}, f32[1,4096]{1,0:T(1,128)S(1)})) conditional(s32[]{:T(128)} %convert_element_type.51, (f32[1,4096,128]{2,1,0:T(8,128)S(1)}, f32[1,4096]{1,0:T(1,128)S(1)}, f32[1,4096]{1,0:T(1,128)S(1)}) %tuple.103, (bf16[512,1024]{1,0:T(8,128)(2,1)}, ...), branch_computations={%region_11.11_spmd, %region_12.16_spmd} | conditional | flops 17106944 | bytes 7613217 | solution.py:81
  819.2 16.2 %conditional.2 = ((f32[1,4096,128]{2,1,0:T(8,128)S(1)}, f32[1,4096]{1,0:T(1,128)S(1)}, f32[1,4096]{1,0:T(1,128)S(1)})) conditional(s32[]{:T(128)} %convert_element_type.51, (f32[1,4096,128]{2,1,0:T(8,128)S(1)}, f32[1,4096]{1,0:T(1,128)S(1)}, f32[1,4096]{1,0:T(1,128)S(1)}) %tuple.103, (bf16[512,1024]{1,0:T(8,128)(2,1)}, ...), branch_computations={%region_11.11_spmd, %region_12.16_spmd} | conditional | flops 17106944 | bytes 7613217 | solution.py:81
  845.6 16.2 %conditional.2 = ((f32[1,4096,128]{2,1,0:T(8,128)S(1)}, f32[1,4096]{1,0:T(1,128)S(1)}, f32[1,4096]{1,0:T(1,128)S(1)})) conditional(s32[]{:T(128)} %convert_element_type.51, (f32[1,4096,128]{2,1,0:T(8,128)S(1)}, f32[1,4096]{1,0:T(1,128)S(1)}, f32[1,4096]{1,0:T(1,128)S(1)}) %tuple.103, (bf16[512,1024]{1,0:T(8,128)(2,1)}, ...), branch_computations={%region_11.11_spmd, %region_12.16_spmd} | conditional | flops 17106944 | bytes 7613217 | solution.py:81
  872.1 16.2 %conditional.2 = ((f32[1,4096,128]{2,1,0:T(8,128)S(1)}, f32[1,4096]{1,0:T(1,128)S(1)}, f32[1,4096]{1,0:T(1,128)S(1)})) conditional(s32[]{:T(128)} %convert_element_type.51, (f32[1,4096,128]{2,1,0:T(8,128)S(1)}, f32[1,4096]{1,0:T(1,128)S(1)}, f32[1,4096]{1,0:T(1,128)S(1)}) %tuple.103, (bf16[512,1024]{1,0:T(8,128)(2,1)}, ...), branch_computations={%region_11.11_spmd, %region_12.16_spmd} | conditional | flops 17106944 | bytes 7613217 | solution.py:81
  898.6 16.2 %conditional.2 = ((f32[1,4096,128]{2,1,0:T(8,128)S(1)}, f32[1,4096]{1,0:T(1,128)S(1)}, f32[1,4096]{1,0:T(1,128)S(1)})) conditional(s32[]{:T(128)} %convert_element_type.51, (f32[1,4096,128]{2,1,0:T(8,128)S(1)}, f32[1,4096]{1,0:T(1,128)S(1)}, f32[1,4096]{1,0:T(1,128)S(1)}) %tuple.103, (bf16[512,1024]{1,0:T(8,128)(2,1)}, ...), branch_computations={%region_11.11_spmd, %region_12.16_spmd} | conditional | flops 17106944 | bytes 7613217 | solution.py:81
  925.0 16.2 %conditional.2 = ((f32[1,4096,128]{2,1,0:T(8,128)S(1)}, f32[1,4096]{1,0:T(1,128)S(1)}, f32[1,4096]{1,0:T(1,128)S(1)})) conditional(s32[]{:T(128)} %convert_element_type.51, (f32[1,4096,128]{2,1,0:T(8,128)S(1)}, f32[1,4096]{1,0:T(1,128)S(1)}, f32[1,4096]{1,0:T(1,128)S(1)}) %tuple.103, (bf16[512,1024]{1,0:T(8,128)(2,1)}, ...), branch_computations={%region_11.11_spmd, %region_12.16_spmd} | conditional | flops 17106944 | bytes 7613217 | solution.py:81
  978.3 16.0 %collective-permute-start.1 = (bf16[64,128]{1,0:T(8,128)(2,1)S(1)}, bf16[64,128]{1,0:T(8,128)(2,1)S(1)}, u32[]{:S(2)}, u32[]{:S(2)}) collective-permute-start(bf16[64,128]{1,0:T(8,128)(2,1)S(1)} %get-tuple-element.965), channel_id=1, source_target_pairs={{0,8},{8,16},{16,24},{24,32},{32,40},{40,48},{48,56},{56,64},{64,7... | collective-permute-start | bytes 49160 | tf_op jit(solution)/shard_map/while/body/eval_jaxpr/ppermute | solution.py:30
  (2510 shorter events, 1137.3 us)
Async XLA Ops:
  6.5 143.7 %all-reduce.3.cloned.1.call-start = ((), (), s32[]{:S(2)}) async-start(), calls=%async_computation | async-start | bytes 262144 | tf_op jit(solution)/shard_map/psum | solution.py:16
  199.4 8.0 collective-permute-start
  227.4 7.9 collective-permute-start
  253.8 7.9 collective-permute-start
  280.3 7.9 collective-permute-start
  306.7 7.9 collective-permute-start
  333.2 7.9 collective-permute-start
  359.7 7.9 collective-permute-start
  386.1 7.9 collective-permute-start
  412.6 7.9 collective-permute-start
  439.0 7.9 collective-permute-start
  465.5 7.9 collective-permute-start
  491.9 7.9 collective-permute-start
  518.4 7.9 collective-permute-start
  544.9 7.9 collective-permute-start
  571.3 7.9 collective-permute-start
  597.8 7.9 collective-permute-start
  624.3 7.9 collective-permute-start
  650.8 7.9 collective-permute-start
  677.2 8.1 collective-permute-start
  703.7 7.9 collective-permute-start
  730.1 7.9 collective-permute-start
  756.6 7.9 collective-permute-start
  783.1 7.9 collective-permute-start
  809.5 7.9 collective-permute-start
  836.0 7.9 collective-permute-start
  862.4 7.9 collective-permute-start
  888.9 7.9 collective-permute-start
  915.4 7.9 collective-permute-start
  952.1 17.9 %collective-permute-start = (bf16[64,128]{1,0:T(8,128)(2,1)}, bf16[64,128]{1,0:T(8,128)(2,1)S(1)}, u32[]{:S(2)}, u32[]{:S(2)}) collective-permute-start(bf16[64,128]{1,0:T(8,128)(2,1)} %get-tuple-element.964), channel_id=1, source_target_pairs={{0,8},{8,16},{16,24},{24,32},{32,40},{40,48},{48,56},{56,64},{64,7... | collective-permute-start | bytes 49160 | tf_op jit(solution)/shard_map/while/body/eval_jaxpr/ppermute | solution.py:30
  976.4 17.9 %collective-permute-start = (bf16[64,128]{1,0:T(8,128)(2,1)}, bf16[64,128]{1,0:T(8,128)(2,1)S(1)}, u32[]{:S(2)}, u32[]{:S(2)}) collective-permute-start(bf16[64,128]{1,0:T(8,128)(2,1)} %get-tuple-element.964), channel_id=1, source_target_pairs={{0,8},{8,16},{16,24},{24,32},{32,40},{40,48},{48,56},{56,64},{64,7... | collective-permute-start | bytes 49160 | tf_op jit(solution)/shard_map/while/body/eval_jaxpr/ppermute | solution.py:30
  978.3 17.4 %collective-permute-start.1 = (bf16[64,128]{1,0:T(8,128)(2,1)S(1)}, bf16[64,128]{1,0:T(8,128)(2,1)S(1)}, u32[]{:S(2)}, u32[]{:S(2)}) collective-permute-start(bf16[64,128]{1,0:T(8,128)(2,1)S(1)} %get-tuple-element.965), channel_id=1, source_target_pairs={{0,8},{8,16},{16,24},{24,32},{32,40},{40,48},{48,56},{56,64},{64,7... | collective-permute-start | bytes 49160 | tf_op jit(solution)/shard_map/while/body/eval_jaxpr/ppermute | solution.py:30
  (37 other events, 253.9 us)
Sparse Core Ops, SparseCore 0:
  10.9 139.3 all-reduce.2
where the time goes:
time: 1020 us; the launch traced here: 1010 us
  waiting for transfers between devices  313 us (31%)
  matrix products  284 us (28%)
  local copies, waits for them, and re-layouts  165 us (16%)
  starting transfers between devices  150 us (15%)
  other arithmetic  58.9 us (6%)
  loops' own time  20 us (2%)
  between operations  13.5 us (1%)
    dot_general x240, matrix products, block(): jnp.dot(weight.astype(jnp.bfloat16), vhead, preferred_element_type=jnp.fl...  228 us
    ppermute x62, waiting for transfers between devices, from_behind(): return lax.ppermute(block, axis, route)  174 us
    ppermute x62, starting transfers between devices, from_behind(): return lax.ppermute(block, axis, route)  150 us
    psum x1, waiting for transfers between devices, broadcast(): return lax.psum(jnp.where(mine, x, jnp.zeros_like(x)), axis)  140 us
    dot_general x240, matrix products, block(): jnp.dot(qblock, khead.T, preferred_element_type=jnp.float32) * scale  54.8 us
    cond x84, local copies, waits for them, and re-layouts  45.6 us
    another operation x29, local copies, waits for them, and re-layouts, fold_head(): qrows.reshape(count, width, -1)  44.1 us
    another operation x140, other arithmetic  37.6 us
  transfers between devices with their start and end apart: 63, of which 61 were waited for; matrix products, arithmetic and copies ran while one was open for 0% of the time, Pallas kernels for 0%

commit v1 on v0

v1 whole, which is shorter than its diff:
```python
import functools

import jax
import jax.numpy as jnp
from jax import lax
from jax.experimental import pallas as pl
from jax.experimental.pallas import tpu as pltpu
from jax.sharding import PartitionSpec as P

HEAD_DIM = 128
QUERY_PER_KV = 8
ANCHOR_TOKENS = 256
TILE = 256
PIECE = 16
LOG2_SCALE = HEAD_DIM**-0.5 * 1.4426950408889634
NEG = -1e30
F32, BF16 = jnp.float32, jnp.bfloat16


def scores_of(q2, k):
    k2 = jnp.concatenate([k, k], axis=1)
    return lax.dot_general(q2, k2, (((1,), (1,)), ((), ())), preferred_element_type=F32)


def weighted(p, v, ones):
    v2 = jnp.concatenate([v, ones], axis=1)
    return jnp.dot(p.astype(BF16), v2, preferred_element_type=F32)


def kernel(hosts, heads, q_hbm, k_ref, v_ref, kept_ref, o_hbm,
           q_buf, q2_buf, kv, ones_buf, mine, anchor, acc, top, o_buf,
           q_sem, o_sem, send_sem, recv_sem, hand_sem, pass_sem, anchor_sem):
    me = lax.axis_index("ctx")
    blk = k_ref.shape[0]
    ret = mine.shape[0]
    half = hosts // 2
    base = hosts * ret
    pieces = ANCHOR_TOKENS // PIECE
    first_relay = hosts // 4
    is_relay = (me >= first_relay) & (me < first_relay + pieces)
    chunks = blk // TILE
    rows = heads * TILE

    load_q = pltpu.make_async_copy(q_hbm, q_buf, q_sem)
    load_q.start()
    barrier = pltpu.get_barrier_semaphore()

    def greet(i, _):
        pl.semaphore_signal(barrier, inc=1, device_id={"ctx": lax.rem(me + i, hosts)},
                            device_id_type=pl.DeviceIdType.MESH)
        return 0

    lax.fori_loop(1, hosts, greet, 0)

    spots = lax.broadcasted_iota(jnp.int32, (blk, ret), 0)
    onehot = (kept_ref[0] == spots).astype(BF16)
    pick = (((0,), (0,)), ((), ()))
    mine[:, :HEAD_DIM] = lax.dot_general(onehot, k_ref[...], pick, preferred_element_type=F32).astype(BF16)
    mine[:, HEAD_DIM:] = lax.dot_general(onehot, v_ref[...], pick, preferred_element_type=F32).astype(BF16)

    @pl.when(me == 0)
    def _():
        anchor[:, :HEAD_DIM] = k_ref[:ANCHOR_TOKENS, :]
        anchor[:, HEAD_DIM:] = v_ref[:ANCHOR_TOKENS, :]

    first_key = jnp.broadcast_to(k_ref[0:1, :], (ret, HEAD_DIM))

    def blank(start):
        kv[pl.ds(start, ret), :HEAD_DIM] = first_key
        kv[pl.ds(start, ret), HEAD_DIM:] = jnp.zeros((ret, HEAD_DIM), BF16)
        ones_buf[pl.ds(start, ret), :] = jnp.zeros((ret, HEAD_DIM), BF16)

    def blank_slot(j, _):
        blank(pl.multiple_of(j * ret, ret))
        return 0

    def one_slot(j, _):
        ones_buf[pl.ds(pl.multiple_of(j * ret, ret), ret), :] = jnp.ones((ret, HEAD_DIM), BF16)
        return 0

    lax.fori_loop(0, me, one_slot, 0)
    lax.fori_loop(me, hosts, blank_slot, 0)

    @pl.when(me == 0)
    def _():
        for j in range(ANCHOR_TOKENS // ret):
            blank(base + j * ret)

    @pl.when(me > 0)
    def _():
        ones_buf[base:, :] = jnp.ones((ANCHOR_TOKENS, HEAD_DIM), BF16)

    pl.semaphore_wait(barrier, hosts - 1)

    def block_to(dst):
        slot = kv.at[pl.ds(pl.multiple_of(me * ret, ret), ret)]
        return pltpu.make_async_remote_copy(
            src_ref=mine, dst_ref=slot, send_sem=send_sem.at[dst], recv_sem=recv_sem.at[me],
            device_id={"ctx": dst}, device_id_type=pl.DeviceIdType.MESH)

    def block_from(src):
        slot = kv.at[pl.ds(pl.multiple_of(src * ret, ret), ret)]
        return pltpu.make_async_remote_copy(
            src_ref=mine, dst_ref=slot, send_sem=send_sem.at[src], recv_sem=recv_sem.at[src],
            device_id={"ctx": src}, device_id_type=pl.DeviceIdType.MESH)

    def hand(p):
        return pltpu.make_async_remote_copy(
            src_ref=anchor.at[pl.ds(pl.multiple_of(p * PIECE, PIECE), PIECE)],
            dst_ref=kv.at[pl.ds(pl.multiple_of(base + p * PIECE, PIECE), PIECE)],
            send_sem=hand_sem.at[p], recv_sem=anchor_sem.at[p],
            device_id={"ctx": first_relay + p}, device_id_type=pl.DeviceIdType.MESH)

    def passed(p, dst):
        piece = kv.at[pl.ds(pl.multiple_of(base + p * PIECE, PIECE), PIECE)]
        return pltpu.make_async_remote_copy(
            src_ref=piece, dst_ref=piece, send_sem=pass_sem.at[dst], recv_sem=anchor_sem.at[p],
            device_id={"ctx": dst}, device_id_type=pl.DeviceIdType.MESH)

    @pl.when(me == 0)
    def _():
        def go(p, _):
            hand(p).start()
            return 0

        lax.fori_loop(0, pieces, go, 0)

    def send(i, _):
        block_to(hosts - 1 - i).start()
        return 0

    lax.fori_loop(0, hosts - 1 - me, send, 0)

    load_q.wait()
    lower = lax.broadcasted_iota(jnp.int32, (TILE, TILE), 0) >= lax.broadcasted_iota(jnp.int32, (TILE, TILE), 1)

    def chunk_rows(c):
        return pl.ds(pl.multiple_of(c * rows, rows), rows)

    def store(c, newtop, newacc):
        top[chunk_rows(c), :] = jnp.broadcast_to(newtop, (rows, HEAD_DIM))
        acc[chunk_rows(c), :] = newacc

    def own(c):
        parts = [q_buf[c * TILE:(c + 1) * TILE, h * HEAD_DIM:(h + 1) * HEAD_DIM] for h in range(heads)]
        x = jnp.concatenate(parts, axis=0).astype(F32) * LOG2_SCALE
        high = x.astype(BF16)
        low = (x - high.astype(F32)).astype(BF16)
        q2 = jnp.concatenate([high, low], axis=1)
        q2_buf[chunk_rows(c), :] = q2
        ones = jnp.ones((TILE, HEAD_DIM), BF16)
        state = None
        for t in range(c, -1, -1):
            s = scores_of(q2, k_ref[t * TILE:(t + 1) * TILE, :])
            if t == c:
                s = jnp.where(jnp.concatenate([lower] * heads, axis=0), s, NEG)
            state = update(state, s, v_ref[t * TILE:(t + 1) * TILE, :], ones)
        store(c, *state)

    def update(state, s, v, ones):
        newtop = jnp.max(s, axis=1, keepdims=True)
        if state is None:
            return newtop, weighted(jnp.exp2(s - newtop), v, ones)
        oldtop, oldacc = state
        newtop = jnp.maximum(oldtop, newtop)
        d = weighted(jnp.exp2(s - newtop), v, ones)
        return newtop, oldacc * jnp.exp2(oldtop - newtop) + d

    def passing(c, tiles):
        q2 = q2_buf[chunk_rows(c), :]
        state = top[chunk_rows(c), 0:1], acc[chunk_rows(c), :]
        for t in tiles:
            at = slice(t * TILE, (t + 1) * TILE)
            state = update(state, scores_of(q2, kv[at, :HEAD_DIM]), kv[at, HEAD_DIM:], ones_buf[at, :])
        return state

    def arrive(lo, hi):
        def one(i, _):
            block_from(hi - 1 - i).wait_recv()
            return 0

        lax.fori_loop(0, hi - lo, one, 0)

    own(0)

    @pl.when(is_relay)
    def _():
        p = me - first_relay
        hand(p).wait_recv()

        def go(i, _):
            dst = lax.rem(me + i, hosts)

            @pl.when(dst > 0)
            def _():
                passed(p, dst).start()

            return 0

        lax.fori_loop(1, hosts, go, 0)

    for c in range(1, chunks):
        own(c)

    tiles = hosts * ret // TILE

    @pl.when(me > half)
    def _():
        arrive(half, me)
        for c in range(chunks):
            store(c, *passing(c, range(tiles - 1, tiles // 2 - 1, -1)))

    arrive(0, jnp.minimum(me, half))

    @pl.when(me > 0)
    def _():
        def one(p, _):
            @pl.when(p + first_relay != me)
            def _():
                hand(p).wait_recv()

            return 0

        lax.fori_loop(0, pieces, one, 0)

    last = list(range(tiles // 2 - 1, -1, -1)) + [tiles + i for i in range(ANCHOR_TOKENS // TILE)]
    outs = []
    for c in range(chunks):
        _, total = passing(c, last)
        o = (total[:, :HEAD_DIM] / total[:, HEAD_DIM:]).astype(BF16)
        for h in range(heads):
            o_buf[c * TILE:(c + 1) * TILE, h * HEAD_DIM:(h + 1) * HEAD_DIM] = o[h * TILE:(h + 1) * TILE]
        at = pl.ds(c * TILE, TILE)
        out = pltpu.make_async_copy(o_buf.at[at], o_hbm.at[at], o_sem.at[c])
        out.start()
        outs.append(out)

    def sent(i, _):
        block_to(hosts - 1 - i).wait_send()
        return 0

    lax.fori_loop(0, hosts - 1 - me, sent, 0)

    @pl.when(me == 0)
    def _():
        def one(p, _):
            hand(p).wait_send()
            return 0

        lax.fori_loop(0, pieces, one, 0)

    @pl.when(is_relay)
    def _():
        def one(i, _):
            dst = lax.rem(me + i, hosts)

            @pl.when(dst > 0)
            def _():
                passed(me - first_relay, dst).wait_send()

            return 0

        lax.fori_loop(1, hosts, one, 0)

    for out in outs:
        out.wait()


def on_device(hosts, queries, keys, values, kept):
    blk, width = queries.shape
    heads = width // HEAD_DIM
    ret = kept.shape[2]
    slots = hosts * ret + ANCHOR_TOKENS
    pieces = ANCHOR_TOKENS // PIECE
    vmem = pl.BlockSpec(memory_space=pltpu.VMEM)
    return pl.pallas_call(
        functools.partial(kernel, hosts, heads),
        out_shape=jax.ShapeDtypeStruct((blk, width), BF16),
        in_specs=[pl.BlockSpec(memory_space=pl.ANY), vmem, vmem, vmem],
        out_specs=pl.BlockSpec(memory_space=pl.ANY),
        scratch_shapes=[
            pltpu.VMEM((blk, width), BF16),
            pltpu.VMEM((blk * heads, 2 * HEAD_DIM), BF16),
            pltpu.VMEM((slots, 2 * HEAD_DIM), BF16),
            pltpu.VMEM((slots, HEAD_DIM), BF16),
            pltpu.VMEM((ret, 2 * HEAD_DIM), BF16),
            pltpu.VMEM((ANCHOR_TOKENS, 2 * HEAD_DIM), BF16),
            pltpu.VMEM((blk * heads, 2 * HEAD_DIM), F32),
            pltpu.VMEM((blk * heads, HEAD_DIM), F32),
            pltpu.VMEM((blk, width), BF16),
            pltpu.SemaphoreType.DMA,
            pltpu.SemaphoreType.DMA((blk // TILE,)),
            pltpu.SemaphoreType.DMA((hosts,)),
            pltpu.SemaphoreType.DMA((hosts,)),
            pltpu.SemaphoreType.DMA((pieces,)),
            pltpu.SemaphoreType.DMA((hosts,)),
            pltpu.SemaphoreType.DMA((pieces,)),
        ],
        compiler_params=pltpu.CompilerParams(
            collective_id=0, has_side_effects=True, vmem_limit_bytes=48 * 2**20),
    )(queries, keys, values, kept[0])


def solution(mesh):
    placed = (P("ctx", "head"), P("ctx", "head"), P("ctx", "head"), P("head", "ctx", None))
    return jax.shard_map(
        functools.partial(on_device, mesh.shape["ctx"]), mesh=mesh, in_specs=placed,
        out_specs=P("ctx", "head"), check_vma=False)
```

time: 1020 us -> 71.2 us (0.07)
  the two profiles are of different devices: /device:TPU:226 before, /device:TPU:164 now
where the time goes in v1:
time: 71.2 us; the launch traced here: 71 us
  Pallas kernels  66.3 us (93%)
  local copies, waits for them, and re-layouts  4.66 us (7%)
    pallas_call x1, Pallas kernels, on_device(): pl.pallas_call(functools.partial(kernel, hosts, heads), out_shape=jax.Sha...  66.3 us
    unnamed x9, local copies, waits for them, and re-layouts  4.66 us

profile of v1, /device:TPU:164, one launch (start us, length us, event | category | flops | bytes accessed | tf_op | source)
XLA Modules:
  0.0 71.0 jit_solution(9130485161829099663)
XLA Ops:
  0.0 0.0 copy-start.3
  0.0 0.7 copy-done.3
  0.7 0.0 copy-start
  0.7 1.2 %copy-done = bf16[512,1024]{1,0:T(8,128)(2,1)S(1)} copy-done((bf16[512,1024]{1,0:T(8,128)(2,1)S(1)}, bf16[512,1024]{1,0:T(8,128)(2,1)}, u32[]{:S(2)}) %copy-start) | copy-done | bytes 1048600
  1.9 0.0 copy-start.1
  1.9 0.9 %copy-done.1 = bf16[512,128]{1,0:T(8,128)(2,1)S(1)} copy-done((bf16[512,128]{1,0:T(8,128)(2,1)S(1)}, bf16[512,128]{1,0:T(8,128)(2,1)}, u32[]{:S(2)}) %copy-start.1) | copy-done | bytes 131096
  2.8 0.0 copy-start.2
  2.8 0.9 %copy-done.2 = bf16[512,128]{1,0:T(8,128)(2,1)S(1)} copy-done((bf16[512,128]{1,0:T(8,128)(2,1)S(1)}, bf16[512,128]{1,0:T(8,128)(2,1)}, u32[]{:S(2)}) %copy-start.2) | copy-done | bytes 131096
  3.7 66.3 %shard_map.46 = bf16[512,1024]{1,0:T(8,128)(2,1)S(1)} custom-call(bf16[512,1024]{1,0:T(8,128)(2,1)S(1)} %copy-done, bf16[512,128]{1,0:T(8,128)(2,1)S(1)} %copy-done.1, bf16[512,128]{1,0:T(8,128)(2,1)S(1)} %copy-done.2, s32[1,64]{1,0:T(1,128)S(1)} %bitcast.1), custom_call_target="tpu_custom_call" | custom-call | tf_op jit(solution)/shard_map/pallas_call | solution.py:276
  70.0 1.0 %copy.6 = bf16[512,1024]{1,0:T(8,128)(2,1)} copy(bf16[512,1024]{1,0:T(8,128)(2,1)S(1)} %shard_map.46) | data formatting | bytes 2097152
Async XLA Ops:
  0.0 0.7 copy-start.3
  0.7 1.2 %copy-start = (bf16[512,1024]{1,0:T(8,128)(2,1)S(1)}, bf16[512,1024]{1,0:T(8,128)(2,1)}, u32[]{:S(2)}) copy-start(bf16[512,1024]{1,0:T(8,128)(2,1)} %q_hbm.1) | copy-start | bytes 3145732
  1.9 0.9 %copy-start.1 = (bf16[512,128]{1,0:T(8,128)(2,1)S(1)}, bf16[512,128]{1,0:T(8,128)(2,1)}, u32[]{:S(2)}) copy-start(bf16[512,128]{1,0:T(8,128)(2,1)} %k_ref.1) | copy-start | bytes 393220
  2.8 0.9 %copy-start.2 = (bf16[512,128]{1,0:T(8,128)(2,1)S(1)}, bf16[512,128]{1,0:T(8,128)(2,1)}, u32[]{:S(2)}) copy-start(bf16[512,128]{1,0:T(8,128)(2,1)} %v_ref.1) | copy-start | bytes 393220

commit v2 on v0

v2 whole, which is shorter than its diff:
```python
import functools

import jax
import jax.numpy as jnp
from jax import lax
from jax.experimental import pallas as pl
from jax.experimental.pallas import tpu as pltpu
from jax.sharding import PartitionSpec as P

HEAD_DIM = 128
ANCHOR_TOKENS = 256
TILE = 256
RING = 4
LOG2_SCALE = HEAD_DIM**-0.5 * 1.4426950408889634
NEG = -1e30
F32, BF16 = jnp.float32, jnp.bfloat16
MESH = pl.DeviceIdType.MESH


def loop(lo, hi, body):
    def step(i, carry):
        body(i)
        return carry

    lax.fori_loop(lo, hi, step, 0)


def scores_of(q2, k):
    k2 = jnp.concatenate([k, k], axis=1)
    return lax.dot_general(q2, k2, (((1,), (1,)), ((), ())), preferred_element_type=F32)


def fold(state, s, v, ones):
    top = jnp.broadcast_to(jnp.max(s, axis=1, keepdims=True), (s.shape[0], HEAD_DIM))
    if state is not None:
        top = jnp.maximum(state[0], top)
    p = jnp.exp2(s - jnp.concatenate([top, top], axis=1)).astype(BF16)
    new = jnp.dot(p, jnp.concatenate([v, ones], axis=1), preferred_element_type=F32)
    if state is not None:
        factor = jnp.exp2(state[0] - top)
        new = state[1] * jnp.concatenate([factor, factor], axis=1) + new
    return top, new


def kernel(rows, heads, q_hbm, k_hbm, v_hbm, kept_hbm, o_ref,
           q_buf, k_buf, v_buf, kept_buf, q2_buf, kv, anchor, row_ones, mine, acc, top,
           in_sem, ready, z_send, a_send, z_recv, y_send, y_recv, h_send, h_recv, r_send, r_recv, hand_send):
    me = lax.axis_index("ctx")
    z, y = me // RING, me % RING
    blk = k_buf.shape[0]
    ret = mine.shape[0]
    half = ret // 2
    mid = rows // 2
    count = blk * heads
    both = heads * TILE
    own_level = rows

    loads = [pltpu.make_async_copy(a, b, in_sem.at[i]) for i, (a, b) in enumerate(
        [(kept_hbm, kept_buf), (k_hbm, k_buf), (v_hbm, v_buf), (q_hbm, q_buf)])]
    for load in loads:
        load.start()

    def at(zz, yy):
        return {"ctx": zz * RING + yy}

    barrier = pltpu.get_barrier_semaphore()
    for d in range(1, RING):
        pl.semaphore_signal(barrier, inc=1, device_id=at(z, (y + d) % RING), device_id_type=MESH)
    loop(z + 1, rows, lambda t: pl.semaphore_signal(barrier, inc=1, device_id=at(t, y), device_id_type=MESH))

    def slot(level, column, first=0, n=None):
        start = pl.multiple_of((level * RING + column) * ret + first, half)
        return kv.at[pl.ds(start, ret if n is None else n)]

    def remote(src, dst, send, recv, to):
        return pltpu.make_async_remote_copy(src_ref=src, dst_ref=dst, send_sem=send, recv_sem=recv,
                                            device_id=to, device_id_type=MESH)

    for load in loads[:3]:
        load.wait()
    spots = lax.broadcasted_iota(jnp.int32, (blk, ret), 0)
    onehot = (kept_buf[...] == spots).astype(BF16)
    pick = (((0,), (0,)), ((), ()))
    mine[:, :HEAD_DIM] = lax.dot_general(onehot, k_buf[...], pick, preferred_element_type=F32).astype(BF16)
    mine[:, HEAD_DIM:] = lax.dot_general(onehot, v_buf[...], pick, preferred_element_type=F32).astype(BF16)

    first_key = jnp.broadcast_to(k_buf[0:1, :], (ret, HEAD_DIM))

    def blank(c):
        r = pl.ds(pl.multiple_of((own_level * RING + c) * ret, ret), ret)
        kv[r, :HEAD_DIM] = first_key
        kv[r, HEAD_DIM:] = jnp.zeros((ret, HEAD_DIM), BF16)
        row_ones[pl.ds(pl.multiple_of(c * ret, ret), ret), :] = jnp.zeros((ret, HEAD_DIM), BF16)

    def filled(c):
        row_ones[pl.ds(pl.multiple_of(c * ret, ret), ret), :] = jnp.ones((ret, HEAD_DIM), BF16)

    loop(0, y, filled)
    loop(y, RING, blank)

    quarter = ANCHOR_TOKENS // RING

    @pl.when(me == 0)
    def _():
        anchor[:, :HEAD_DIM] = k_buf[:ANCHOR_TOKENS, :]
        anchor[:, HEAD_DIM:] = v_buf[:ANCHOR_TOKENS, :]
        kv[:quarter, :] = anchor[:quarter, :]

    def own():
        loads[3].wait()
        ones = jnp.ones((TILE, HEAD_DIM), BF16)
        lower = lax.broadcasted_iota(jnp.int32, (TILE, TILE), 0) >= lax.broadcasted_iota(jnp.int32, (TILE, TILE), 1)
        lower = jnp.concatenate([lower] * heads, axis=0)
        for c in range(blk // TILE):
            r = slice(c * both, (c + 1) * both)
            for h in range(heads):
                x = q_buf[c * TILE:(c + 1) * TILE, h * HEAD_DIM:(h + 1) * HEAD_DIM].astype(F32) * LOG2_SCALE
                high = x.astype(BF16)
                low = (x - high.astype(F32)).astype(BF16)
                q2_buf[c * both + h * TILE:c * both + (h + 1) * TILE, :] = jnp.concatenate([high, low], axis=1)
            q2 = q2_buf[r, :]
            state = None
            for t in range(c, -1, -1):
                s = scores_of(q2, k_buf[t * TILE:(t + 1) * TILE, :])
                if t == c:
                    s = jnp.where(lower, s, NEG)
                state = fold(state, s, v_buf[t * TILE:(t + 1) * TILE, :], ones)
            top[r, :], acc[r, :] = state

    def level_keys(level):
        tile = kv[pl.ds(pl.multiple_of(level * TILE, TILE), TILE), :]
        return tile[:, :HEAD_DIM], tile[:, HEAD_DIM:]

    def compute(level, ones):
        k, v = level_keys(level)
        top[...], acc[...] = fold((top[...], acc[...]), scores_of(q2_buf[...], k), v, ones)

    early = y < RING // 2

    @pl.when(early)
    def _():
        own()

    pl.semaphore_wait(barrier, z + RING - 1)
    loop(0, z, lambda t: pl.semaphore_signal(ready.at[z], inc=1, device_id=at(t, y), device_id_type=MESH))

    def hand(a):
        return remote(anchor.at[pl.ds(a * quarter, quarter)], slot(0, a), hand_send.at[a], z_recv.at[0], at(0, a))

    def to_row(c):
        return remote(mine, slot(own_level, y), r_send.at[c], r_recv.at[y], at(z, c))

    def from_row(c):
        return remote(mine, slot(own_level, c), r_send.at[c], r_recv.at[c], at(z, c))

    @pl.when(me == 0)
    def _():
        for a in range(1, RING):
            hand(a).start()

    loop(y + 1, RING, lambda c: to_row(c).start())

    def down(t):
        return remote(mine, slot(z + 1, y), z_send.at[t], z_recv.at[z + 1], at(t, y))

    def down_anchor(t):
        return remote(slot(0, y), slot(0, y), a_send.at[t], z_recv.at[0], at(t, y))

    def from_above(level):
        return remote(mine, slot(level, y), z_send.at[0], z_recv.at[level], at(z, (y + 1) % RING))

    @pl.when((z == 0) & (y > 0))
    def _():
        from_above(0).wait_recv()

    def send_down(t):
        pl.semaphore_wait(ready.at[t], 1)
        down(t).start()

        @pl.when(z == 0)
        def _():
            down_anchor(t).start()

    loop(z + 1, mid, send_down)
    last = rows - 1
    loop(0, jnp.minimum(last - z, rows - mid), lambda i: send_down(last - i))

    @pl.when(jnp.logical_not(early))
    def _():
        own()

    right, left, far = (y + 1) % RING, (y + RING - 1) % RING, (y + 2) % RING

    def level_of(i):
        h = i // 2
        return h + (1 - i % 2) * (z - 2 * h)

    def to_right(l):
        return remote(slot(l, y), slot(l, y), y_send.at[0, l], y_recv.at[0, l], at(z, right))

    def to_left(l):
        return remote(slot(l, y), slot(l, y), y_send.at[1, l], y_recv.at[1, l], at(z, left))

    def from_left(l):
        return remote(slot(l, left), slot(l, left), y_send.at[0, l], y_recv.at[0, l], at(z, left))

    def from_right(l):
        return remote(slot(l, right), slot(l, right), y_send.at[1, l], y_recv.at[1, l], at(z, right))

    def on_right(l):
        part = slot(l, left, 0, half)
        return remote(part, part, h_send.at[0, l], h_recv.at[0, l], at(z, right))

    def on_left(l):
        part = slot(l, right, half, half)
        return remote(part, part, h_send.at[1, l], h_recv.at[1, l], at(z, left))

    def far_left(l):
        part = slot(l, far, 0, half)
        return remote(part, part, h_send.at[0, l], h_recv.at[0, l], at(z, left))

    def far_right(l):
        part = slot(l, far, half, half)
        return remote(part, part, h_send.at[1, l], h_recv.at[1, l], at(z, right))

    def first(i):
        l = level_of(i)

        @pl.when(z > 0)
        def _():
            from_above(l).wait_recv()

        to_right(l).start()
        to_left(l).start()

    def second(i):
        l = level_of(i)
        from_left(l).wait_recv()
        on_right(l).start()
        from_right(l).wait_recv()
        on_left(l).start()

    def third(i):
        l = level_of(i)
        far_left(l).wait_recv()
        far_right(l).wait_recv()

    first(0)

    @pl.when(z > 0)
    def _():
        first(1)

    @pl.when(y > 0)
    def _():
        loop(0, y, lambda c: from_row(c).wait_recv())
        compute(own_level, row_ones[...])

    second(0)

    def step(i):
        @pl.when(i + 2 <= z)
        def _():
            first(i + 2)

        @pl.when(i + 1 <= z)
        def _():
            second(i + 1)

        third(i)

        @pl.when(me > 0)
        def _():
            compute(level_of(i), jnp.ones((TILE, HEAD_DIM), BF16))

    loop(0, z + 1, step)

    for c in range(blk // TILE):
        for h in range(heads):
            r = slice(c * both + h * TILE, c * both + (h + 1) * TILE)
            o_ref[c * TILE:(c + 1) * TILE, h * HEAD_DIM:(h + 1) * HEAD_DIM] = (
                acc[r, :HEAD_DIM] / acc[r, HEAD_DIM:]).astype(BF16)

    def gone(i):
        l = level_of(i)
        for copy in (to_right(l), to_left(l), on_right(l), on_left(l)):
            copy.wait_send()

    loop(0, z + 1, gone)
    loop(y + 1, RING, lambda c: to_row(c).wait_send())
    loop(z + 1, rows, lambda t: down(t).wait_send())

    @pl.when(z == 0)
    def _():
        loop(1, rows, lambda t: down_anchor(t).wait_send())

    @pl.when(me == 0)
    def _():
        for a in range(1, RING):
            hand(a).wait_send()


def on_device(hosts, queries, keys, values, kept):
    blk, width = queries.shape
    heads = width // HEAD_DIM
    ret = kept.shape[2]
    rows = hosts // RING
    hbm = pl.BlockSpec(memory_space=pltpu.HBM)
    dma = pltpu.SemaphoreType.DMA
    return pl.pallas_call(
        functools.partial(kernel, rows, heads),
        out_shape=pltpu.VMEM((blk, width), BF16),
        in_specs=[hbm] * 4,
        out_specs=pl.BlockSpec(memory_space=pltpu.VMEM),
        scratch_shapes=[
            pltpu.VMEM((blk, width), BF16),
            pltpu.VMEM((blk, HEAD_DIM), BF16),
            pltpu.VMEM((blk, HEAD_DIM), BF16),
            pltpu.VMEM((1, ret), jnp.int32),
            pltpu.VMEM((blk * heads, 2 * HEAD_DIM), BF16),
            pltpu.VMEM(((rows + 1) * TILE, 2 * HEAD_DIM), BF16),
            pltpu.VMEM((ANCHOR_TOKENS, 2 * HEAD_DIM), BF16),
            pltpu.VMEM((TILE, HEAD_DIM), BF16),
            pltpu.VMEM((ret, 2 * HEAD_DIM), BF16),
            pltpu.VMEM((blk * heads, 2 * HEAD_DIM), F32),
            pltpu.VMEM((blk * heads, HEAD_DIM), F32),
            dma((4,)),
            pltpu.SemaphoreType.REGULAR((rows,)),
            dma((rows,)), dma((rows,)), dma((rows,)),
            dma((2, rows)), dma((2, rows)), dma((2, rows)), dma((2, rows)),
            dma((RING,)), dma((RING,)), dma((RING,)),
        ],
        compiler_params=pltpu.CompilerParams(
            collective_id=0, has_side_effects=True, vmem_limit_bytes=61 * 2**20),
    )(queries, keys, values, kept[0])


def solution(mesh):
    placed = (P("ctx", "head"), P("ctx", "head"), P("ctx", "head"), P("head", "ctx", None))
    return jax.shard_map(
        functools.partial(on_device, mesh.shape["ctx"]), mesh=mesh, in_specs=placed,
        out_specs=P("ctx", "head"), check_vma=False)
```

time: 1020 us -> 40.7 us (0.04); the launches traced: 1010 us -> 40.6 us
  waiting for transfers between devices: 313 us -> 0 us
  matrix products: 284 us -> 0 us
  local copies, waits for them, and re-layouts: 165 us -> 0.97 us
  starting transfers between devices: 150 us -> 0 us
  other arithmetic: 58.9 us -> 0 us
  Pallas kernels: 0 us -> 39.6 us
  loops' own time: 20 us -> 0 us
  between operations: 13.5 us -> 0.01 us
    dot_general x482 -> x0, matrix products: 284 us -> none  [the longest x240 228 us: block(): jnp.dot(weight.astype(jnp.bfloat16), vhead, preferred_element_type=jnp.fl...]
    ppermute x62 -> x0, waiting for transfers between devices: 174 us -> none  [from_behind(): return lax.ppermute(block, axis, route)]
    ppermute x62 -> x0, starting transfers between devices: 150 us -> none  [from_behind(): return lax.ppermute(block, axis, route)]
    psum x1 -> x0, waiting for transfers between devices: 140 us -> none  [broadcast(): return lax.psum(jnp.where(mine, x, jnp.zeros_like(x)), axis)]
    another operation x63 -> x0, local copies, waits for them, and re-layouts: 61.8 us -> none  [the longest x29 44.1 us: fold_head(): qrows.reshape(count, width, -1)]
    cond x84 -> x0, local copies, waits for them, and re-layouts: 45.6 us -> none
    pallas_call x0 -> x1, Pallas kernels: none -> 39.6 us  [on_device(): pl.pallas_call(functools.partial(kernel, rows, heads), out_shape=pltpu.VM...]
    another operation x140 -> x0, other arithmetic: 37.6 us -> none
  transfers between devices with their start and end apart: 63 -> 0, of which waited for: 61 -> 0; matrix products, arithmetic and copies ran while one was open for 0% -> 0% of each run, Pallas kernels for 0% -> 0%
where the time goes in v2:
time: 40.7 us; the launch traced here: 40.6 us
  Pallas kernels  39.6 us (97%)
  local copies, waits for them, and re-layouts  0.97 us (2%)
    pallas_call x1, Pallas kernels, on_device(): pl.pallas_call(functools.partial(kernel, rows, heads), out_shape=pltpu.VM...  39.6 us
    unnamed x1, local copies, waits for them, and re-layouts  0.97 us

profile of v2, /device:TPU:226, one launch (start us, length us, event | category | flops | bytes accessed | tf_op | source)
XLA Modules:
  0.0 40.6 jit_solution(4298429687017411478)
XLA Ops:
  0.0 39.6 %shard_map.46 = bf16[512,1024]{1,0:T(8,128)(2,1)S(1)} custom-call(bf16[512,1024]{1,0:T(8,128)(2,1)} %q_hbm.1, bf16[512,128]{1,0:T(8,128)(2,1)} %k_hbm.1, bf16[512,128]{1,0:T(8,128)(2,1)} %v_hbm.1, s32[1,64]{1,0:T(1,128)} %bitcast.1), custom_call_target="tpu_custom_call" | custom-call | tf_op jit(solution)/shard_map/pallas_call | solution.py:310
  39.6 1.0 %copy.6 = bf16[512,1024]{1,0:T(8,128)(2,1)} copy(bf16[512,1024]{1,0:T(8,128)(2,1)S(1)} %shard_map.46) | data formatting | bytes 2097152

commit v3 on v2

v3 whole, which is shorter than its diff:
```python
import functools

import jax
import jax.numpy as jnp
from jax import lax
from jax.experimental import pallas as pl
from jax.experimental.pallas import tpu as pltpu
from jax.sharding import PartitionSpec as P

HEAD_DIM = 128
ANCHOR_TOKENS = 256
TILE = 256
AHEAD = 4
RING = 4
LOG2_SCALE = HEAD_DIM**-0.5 * 1.4426950408889634
NEG = -1e30
F32, BF16 = jnp.float32, jnp.bfloat16
MESH = pl.DeviceIdType.MESH


def loop(lo, hi, body):
    def step(i, carry):
        body(i)
        return carry

    lax.fori_loop(lo, hi, step, 0)


def scores_of(q2, k):
    k2 = jnp.concatenate([k, k], axis=1)
    return lax.dot_general(q2, k2, (((1,), (1,)), ((), ())), preferred_element_type=F32)


def fold(state, s, v, ones):
    top = jnp.broadcast_to(jnp.max(s, axis=1, keepdims=True), (s.shape[0], HEAD_DIM))
    if state is not None:
        top = jnp.maximum(state[0], top)
    p = jnp.exp2(s - jnp.concatenate([top, top], axis=1)).astype(BF16)
    new = jnp.dot(p, jnp.concatenate([v, ones], axis=1), preferred_element_type=F32)
    if state is not None:
        factor = jnp.exp2(state[0] - top)
        new = state[1] * jnp.concatenate([factor, factor], axis=1) + new
    return top, new


def kernel(rows, heads, q_hbm, k_hbm, v_hbm, kept_hbm, o_ref,
           q_buf, k_buf, v_buf, kept_buf, q2_buf, kv, anchor, ones, mine, acc, top,
           in_sem, z_send, z_recv, y_send, y_recv, r_send, r_recv, hand_send, a_recv, a_send, ay_send, ay_recv):
    me = lax.axis_index("ctx")
    z, y = me // RING, me % RING
    blk = k_buf.shape[0]
    ret = mine.shape[0]
    both = heads * TILE
    last = rows - 1

    loads = [pltpu.make_async_copy(a, b, in_sem.at[i]) for i, (a, b) in enumerate(
        [(kept_hbm, kept_buf), (k_hbm, k_buf), (v_hbm, v_buf), (q_hbm, q_buf)])]
    for load in loads:
        load.start()

    def at(zz, yy):
        return {"ctx": zz * RING + yy}

    barrier = pltpu.get_barrier_semaphore()
    loop(0, z, lambda t: pl.semaphore_signal(barrier, inc=1, device_id=at(t, y), device_id_type=MESH))
    for d in range(1, RING):
        pl.semaphore_signal(barrier, inc=1, device_id=at(z, (y + d) % RING), device_id_type=MESH)

    def slot(n):
        return kv.at[pl.ds(pl.multiple_of(n * ret, ret), ret)]

    def column_slot(i):
        return slot(RING + i)

    def cross_slot(i, d):
        return slot(RING + z + (RING - 1) * i + d - 1)

    def remote(src, dst, send, recv, to):
        return pltpu.make_async_remote_copy(src_ref=src, dst_ref=dst, send_sem=send, recv_sem=recv,
                                            device_id=to, device_id_type=MESH)

    for load in loads[:3]:
        load.wait()
    spots = lax.broadcasted_iota(jnp.int32, (blk, ret), 0)
    onehot = (kept_buf[...] == spots).astype(BF16)
    pick = (((0,), (0,)), ((), ()))
    mine[:, :HEAD_DIM] = lax.dot_general(onehot, k_buf[...], pick, preferred_element_type=F32).astype(BF16)
    mine[:, HEAD_DIM:] = lax.dot_general(onehot, v_buf[...], pick, preferred_element_type=F32).astype(BF16)

    first_key = jnp.broadcast_to(k_buf[0:1, :], (ret, HEAD_DIM))
    ones[...] = jnp.ones(ones.shape, BF16)

    def blank(c):
        r = pl.ds(pl.multiple_of(c * ret, ret), ret)
        kv[r, :HEAD_DIM] = first_key
        kv[r, HEAD_DIM:] = jnp.zeros((ret, HEAD_DIM), BF16)
        ones[r, :] = jnp.zeros((ret, HEAD_DIM), BF16)

    loop(y, RING, blank)

    quarter = ANCHOR_TOKENS // RING

    @pl.when(me == 0)
    def _():
        anchor[:, :HEAD_DIM] = k_buf[:ANCHOR_TOKENS, :]
        anchor[:, HEAD_DIM:] = v_buf[:ANCHOR_TOKENS, :]
        kv[RING * ret:RING * ret + quarter, :] = anchor[:quarter, :]

    loads[3].wait()
    lower = lax.broadcasted_iota(jnp.int32, (TILE, TILE), 0) >= lax.broadcasted_iota(jnp.int32, (TILE, TILE), 1)
    lower = jnp.concatenate([lower] * heads, axis=0)
    for c in range(blk // TILE):
        r = slice(c * both, (c + 1) * both)
        for h in range(heads):
            x = q_buf[c * TILE:(c + 1) * TILE, h * HEAD_DIM:(h + 1) * HEAD_DIM].astype(F32) * LOG2_SCALE
            high = x.astype(BF16)
            low = (x - high.astype(F32)).astype(BF16)
            q2_buf[c * both + h * TILE:c * both + (h + 1) * TILE, :] = jnp.concatenate([high, low], axis=1)
        q2 = q2_buf[r, :]
        state = None
        for t in range(c, -1, -1):
            s = scores_of(q2, k_buf[t * TILE:(t + 1) * TILE, :])
            if t == c:
                s = jnp.where(lower, s, NEG)
            state = fold(state, s, v_buf[t * TILE:(t + 1) * TILE, :], jnp.ones((TILE, HEAD_DIM), BF16))
        top[r, :], acc[r, :] = state

    def compute(tiles):
        state = top[...], acc[...]
        for t in tiles:
            r = pl.ds(pl.multiple_of(t * TILE, TILE), TILE)
            state = fold(state, scores_of(q2_buf[...], kv[r, :HEAD_DIM]), kv[r, HEAD_DIM:], ones[r, :])
        top[...], acc[...] = state

    pl.semaphore_wait(barrier, last - z + RING - 1)

    def hand(a):
        return remote(anchor.at[pl.ds(a * quarter, quarter)], slot(RING + a), hand_send.at[a], a_recv.at[0], at(0, a))

    def to_row(c):
        return remote(mine, slot(y), r_send.at[c], r_recv.at[y], at(z, c))

    def from_row(c):
        return remote(mine, slot(c), r_send.at[c], r_recv.at[c], at(z, c))

    def down(t):
        return remote(mine, column_slot(t - 1 - z), z_send.at[t], z_recv.at[t - 1 - z], at(t, y))

    def from_above(i):
        return remote(mine, column_slot(i), z_send.at[0], z_recv.at[i], at(z - 1 - i, y))

    def down_anchor(t):
        return remote(slot(RING + y), slot(RING * (t + 1) + y), a_send.at[t], a_recv.at[0], at(t, y))

    def my_anchor():
        quarter_slot = slot(RING * (z + 1) + y)
        return remote(quarter_slot, quarter_slot, a_send.at[0], a_recv.at[0], at(z, (y + 1) % RING))

    def across(i, d):
        return remote(column_slot(i), cross_slot(i, d), y_send.at[d, i], y_recv.at[d, i], at(z, (y + d) % RING))

    def from_across(i, d):
        return remote(column_slot(i), cross_slot(i, d), y_send.at[d, i], y_recv.at[d, i], at(z, (y + RING - d) % RING))

    def across_anchor(d):
        quarter_slot = slot(RING * (z + 1) + y)
        return remote(quarter_slot, quarter_slot, ay_send.at[d], ay_recv.at[d], at(z, (y + d) % RING))

    def from_across_anchor(d):
        there = (y + RING - d) % RING
        quarter_slot = slot(RING * (z + 1) + there)
        return remote(quarter_slot, quarter_slot, ay_send.at[d], ay_recv.at[d], at(z, there))

    @pl.when(me == 0)
    def _():
        for a in range(1, RING):
            hand(a).start()

    loop(0, last - z, lambda i: down(last - i).start())
    loop(y + 1, RING, lambda c: to_row(c).start())

    @pl.when(z == 0)
    def _():
        @pl.when(y > 0)
        def _():
            my_anchor().wait_recv()

        loop(0, last, lambda i: down_anchor(last - i).start())

    def forward(i):
        from_above(i).wait_recv()
        for d in (2, 1, 3):
            across(i, d).start()

    def forward_anchor():
        @pl.when(z > 0)
        def _():
            my_anchor().wait_recv()

        for d in (2, 1, 3):
            across_anchor(d).start()

    def need(t):
        @pl.when(t == 0)
        def _():
            loop(0, y, lambda c: from_row(c).wait_recv())

        @pl.when((t > 0) & (t <= z))
        def _():
            def one(k):
                u = RING * (t - 1) + k - z

                @pl.when(u >= 0)
                def _():
                    from_across(u // (RING - 1), 1 + u % (RING - 1)).wait_recv()

            loop(0, RING, one)

        @pl.when(t == z + 1)
        def _():
            for d in range(1, RING):
                from_across_anchor(d).wait_recv()

    def pair(p):
        loop(jnp.minimum(z, AHEAD * p), jnp.minimum(z, AHEAD * (p + 1)), forward)

        @pl.when(p == jnp.maximum(z // 2 - 1, 0))
        def _():
            forward_anchor()

        need(2 * p)
        need(2 * p + 1)

        @pl.when(me > 0)
        def _():
            compute([2 * p, 2 * p + 1])

    loop(0, (z + 2) // 2, pair)

    @pl.when(z % 2 == 1)
    def _():
        need(z + 1)
        compute([z + 1])

    for c in range(blk // TILE):
        for h in range(heads):
            r = slice(c * both + h * TILE, c * both + (h + 1) * TILE)
            o_ref[c * TILE:(c + 1) * TILE, h * HEAD_DIM:(h + 1) * HEAD_DIM] = (
                acc[r, :HEAD_DIM] / acc[r, HEAD_DIM:]).astype(BF16)

    def gone(i):
        for d in range(1, RING):
            across(i, d).wait_send()

    loop(0, z, gone)
    for d in range(1, RING):
        across_anchor(d).wait_send()
    loop(y + 1, RING, lambda c: to_row(c).wait_send())
    loop(z + 1, rows, lambda t: down(t).wait_send())

    @pl.when(z == 0)
    def _():
        loop(1, rows, lambda t: down_anchor(t).wait_send())

    @pl.when(me == 0)
    def _():
        for a in range(1, RING):
            hand(a).wait_send()


def on_device(hosts, queries, keys, values, kept):
    blk, width = queries.shape
    heads = width // HEAD_DIM
    ret = kept.shape[2]
    rows = hosts // RING
    hbm = pl.BlockSpec(memory_space=pltpu.HBM)
    dma = pltpu.SemaphoreType.DMA
    return pl.pallas_call(
        functools.partial(kernel, rows, heads),
        out_shape=pltpu.VMEM((blk, width), BF16),
        in_specs=[hbm] * 4,
        out_specs=pl.BlockSpec(memory_space=pltpu.VMEM),
        scratch_shapes=[
            pltpu.VMEM((blk, width), BF16),
            pltpu.VMEM((blk, HEAD_DIM), BF16),
            pltpu.VMEM((blk, HEAD_DIM), BF16),
            pltpu.VMEM((1, ret), jnp.int32),
            pltpu.VMEM((blk * heads, 2 * HEAD_DIM), BF16),
            pltpu.VMEM(((rows + 1) * TILE, 2 * HEAD_DIM), BF16),
            pltpu.VMEM((ANCHOR_TOKENS, 2 * HEAD_DIM), BF16),
            pltpu.VMEM(((rows + 1) * TILE, HEAD_DIM), BF16),
            pltpu.VMEM((ret, 2 * HEAD_DIM), BF16),
            pltpu.VMEM((blk * heads, 2 * HEAD_DIM), F32),
            pltpu.VMEM((blk * heads, HEAD_DIM), F32),
            dma((4,)),
            dma((rows,)), dma((rows,)), dma((RING, rows)), dma((RING, rows)),
            dma((RING,)), dma((RING,)), dma((RING,)),
            dma((1,)), dma((rows,)), dma((RING,)), dma((RING,)),
        ],
        compiler_params=pltpu.CompilerParams(
            collective_id=0, has_side_effects=True, vmem_limit_bytes=61 * 2**20),
    )(queries, keys, values, kept[0])


def solution(mesh):
    placed = (P("ctx", "head"), P("ctx", "head"), P("ctx", "head"), P("head", "ctx", None))
    return jax.shard_map(
        functools.partial(on_device, mesh.shape["ctx"]), mesh=mesh, in_specs=placed,
        out_specs=P("ctx", "head"), check_vma=False)
```

time: 40.7 us -> 29.7 us (0.73)
  the two profiles are of different devices: /device:TPU:226 before, /device:TPU:102 now
where the time goes in v3:
time: 29.7 us; the launch traced here: 29.6 us
  Pallas kernels  28.6 us (96%)
  local copies, waits for them, and re-layouts  0.97 us (3%)
    pallas_call x1, Pallas kernels, on_device(): pl.pallas_call(functools.partial(kernel, rows, heads), out_shape=pltpu.VM...  28.6 us
    unnamed x1, local copies, waits for them, and re-layouts  0.97 us

profile of v3, /device:TPU:102, one launch (start us, length us, event | category | flops | bytes accessed | tf_op | source)
XLA Modules:
  0.0 29.6 jit_solution(18346488217978729786)
XLA Ops:
  0.0 28.6 %shard_map.46 = bf16[512,1024]{1,0:T(8,128)(2,1)S(1)} custom-call(bf16[512,1024]{1,0:T(8,128)(2,1)} %q_hbm.1, bf16[512,128]{1,0:T(8,128)(2,1)} %k_hbm.1, bf16[512,128]{1,0:T(8,128)(2,1)} %v_hbm.1, s32[1,64]{1,0:T(1,128)} %bitcast.1), custom_call_target="tpu_custom_call" | custom-call | tf_op jit(solution)/shard_map/pallas_call | solution.py:278
  28.6 1.0 %copy.6 = bf16[512,1024]{1,0:T(8,128)(2,1)} copy(bf16[512,1024]{1,0:T(8,128)(2,1)S(1)} %shard_map.46) | data formatting | bytes 2097152

commit v4 on v3

--- a/solution.py
+++ b/solution.py
@@ -11,6 +11,7 @@
 ANCHOR_TOKENS = 256
 TILE = 256
 AHEAD = 4
+NEAR = 2
 RING = 4
 LOG2_SCALE = HEAD_DIM**-0.5 * 1.4426950408889634
 NEG = -1e30
@@ -44,8 +45,8 @@
 
 
 def kernel(rows, heads, q_hbm, k_hbm, v_hbm, kept_hbm, o_ref,
-           q_buf, k_buf, v_buf, kept_buf, q2_buf, kv, anchor, ones, mine, acc, top,
-           in_sem, z_send, z_recv, y_send, y_recv, r_send, r_recv, hand_send, a_recv, a_send, ay_send, ay_recv):
+           q_buf, k_buf, v_buf, kept_buf, q2_buf, kv, anchor, ones, mine, other, acc, top,
+           in_sem, ready, z_send, z_recv, y_send, y_recv, r_send, r_recv, s_sem, f_send, hand_send, a_recv, a_send, ay_send, ay_recv):
     me = lax.axis_index("ctx")
     z, y = me // RING, me % RING
     blk = k_buf.shape[0]
@@ -62,7 +63,12 @@
         return {"ctx": zz * RING + yy}
 
     barrier = pltpu.get_barrier_semaphore()
-    loop(0, z, lambda t: pl.semaphore_signal(barrier, inc=1, device_id=at(t, y), device_id_type=MESH))
+    loop(1, z, lambda t: pl.semaphore_signal(barrier, inc=1, device_id=at(t, y), device_id_type=MESH))
+
+    @pl.when(z == 0)
+    def _():
+        loop(1, rows, lambda t: pl.semaphore_signal(barrier, inc=1, device_id=at(t, y), device_id_type=MESH))
+
     for d in range(1, RING):
         pl.semaphore_signal(barrier, inc=1, device_id=at(z, (y + d) % RING), device_id_type=MESH)
 
@@ -106,24 +112,25 @@
         anchor[:, HEAD_DIM:] = v_buf[:ANCHOR_TOKENS, :]
         kv[RING * ret:RING * ret + quarter, :] = anchor[:quarter, :]
 
-    loads[3].wait()
-    lower = lax.broadcasted_iota(jnp.int32, (TILE, TILE), 0) >= lax.broadcasted_iota(jnp.int32, (TILE, TILE), 1)
-    lower = jnp.concatenate([lower] * heads, axis=0)
-    for c in range(blk // TILE):
-        r = slice(c * both, (c + 1) * both)
-        for h in range(heads):
-            x = q_buf[c * TILE:(c + 1) * TILE, h * HEAD_DIM:(h + 1) * HEAD_DIM].astype(F32) * LOG2_SCALE
-            high = x.astype(BF16)
-            low = (x - high.astype(F32)).astype(BF16)
-            q2_buf[c * both + h * TILE:c * both + (h + 1) * TILE, :] = jnp.concatenate([high, low], axis=1)
-        q2 = q2_buf[r, :]
-        state = None
-        for t in range(c, -1, -1):
-            s = scores_of(q2, k_buf[t * TILE:(t + 1) * TILE, :])
-            if t == c:
-                s = jnp.where(lower, s, NEG)
-            state = fold(state, s, v_buf[t * TILE:(t + 1) * TILE, :], jnp.ones((TILE, HEAD_DIM), BF16))
-        top[r, :], acc[r, :] = state
+    def own_block():
+        loads[3].wait()
+        lower = lax.broadcasted_iota(jnp.int32, (TILE, TILE), 0) >= lax.broadcasted_iota(jnp.int32, (TILE, TILE), 1)
+        lower = jnp.concatenate([lower] * heads, axis=0)
+        for c in range(blk // TILE):
+            r = slice(c * both, (c + 1) * both)
+            for h in range(heads):
+                x = q_buf[c * TILE:(c + 1) * TILE, h * HEAD_DIM:(h + 1) * HEAD_DIM].astype(F32) * LOG2_SCALE
+                high = x.astype(BF16)
+                low = (x - high.astype(F32)).astype(BF16)
+                q2_buf[c * both + h * TILE:c * both + (h + 1) * TILE, :] = jnp.concatenate([high, low], axis=1)
+            q2 = q2_buf[r, :]
+            state = None
+            for t in range(c, -1, -1):
+                s = scores_of(q2, k_buf[t * TILE:(t + 1) * TILE, :])
+                if t == c:
+                    s = jnp.where(lower, s, NEG)
+                state = fold(state, s, v_buf[t * TILE:(t + 1) * TILE, :], jnp.ones((TILE, HEAD_DIM), BF16))
+            top[r, :], acc[r, :] = state
 
     def compute(tiles):
         state = top[...], acc[...]
@@ -132,7 +139,14 @@
             state = fold(state, scores_of(q2_buf[...], kv[r, :HEAD_DIM]), kv[r, HEAD_DIM:], ones[r, :])
         top[...], acc[...] = state
 
-    pl.semaphore_wait(barrier, last - z + RING - 1)
+    swap = remote(mine, other, s_sem.at[0], s_sem.at[1], at(z, (y + 2) % RING))
+
+    def down_far(i):
+        far = slot(RING + z + 1 + i + (RING - 1) * i + 1)
+        return remote(other, far, f_send.at[i], y_recv.at[2, i], at(z + 1 + i, y))
+
+    def far_from_above(i):
+        return remote(other, cross_slot(i, 2), f_send.at[i], y_recv.at[2, i], at(z - 1 - i, y))
 
     def hand(a):
         return remote(anchor.at[pl.ds(a * quarter, quarter)], slot(RING + a), hand_send.at[a], a_recv.at[0], at(0, a))
@@ -171,25 +185,59 @@
         quarter_slot = slot(RING * (z + 1) + there)
         return remote(quarter_slot, quarter_slot, ay_send.at[d], ay_recv.at[d], at(z, there))
 
-    @pl.when(me == 0)
-    def _():
-        for a in range(1, RING):
-            hand(a).start()
-
+    early = z < rows // 2
+
+    @pl.when(z == 0)
+    def _():
+        pl.semaphore_wait(barrier, RING - 1)
+
+        @pl.when(y == 0)
+        def _():
+            for a in range(1, RING):
+                hand(a).start()
+
+    @pl.when(early)
+    def _():
+        own_block()
+
+    @pl.when(z == 0)
+    def _():
+        @pl.when(y > 0)
+        def _():
+            my_anchor().wait_recv()
+
+        pl.semaphore_wait(ready, last)
+
+    @pl.when(z > 0)
+    def _():
+        pl.semaphore_wait(barrier, last - z + RING)
+        pl.semaphore_signal(ready, inc=1, device_id=at(0, y), device_id_type=MESH)
+
+    swap.start()
     loop(0, last - z, lambda i: down(last - i).start())
+
+    @pl.when(z == 0)
+    def _():
+        loop(0, last, lambda i: down_anchor(last - i).start())
+
     loop(y + 1, RING, lambda c: to_row(c).start())
 
-    @pl.when(z == 0)
-    def _():
-        @pl.when(y > 0)
-        def _():
-            my_anchor().wait_recv()
-
-        loop(0, last, lambda i: down_anchor(last - i).start())
+    @pl.when(jnp.logical_not(early))
+    def _():
+        own_block()
+
+    swap.wait_recv()
+    near = jnp.minimum(NEAR, last - z)
+    loop(0, near, lambda i: down_far(i).start())
 
     def forward(i):
         from_above(i).wait_recv()
-        for d in (2, 1, 3):
+
+        @pl.when(i >= NEAR)
+        def _():
+            across(i, 2).start()
+
+        for d in (1, 3):
             across(i, d).start()
 
     def forward_anchor():
@@ -224,23 +272,36 @@
     def pair(p):
         loop(jnp.minimum(z, AHEAD * p), jnp.minimum(z, AHEAD * (p + 1)), forward)
 
-        @pl.when(p == jnp.maximum(z // 2 - 1, 0))
+        @pl.when(p == jnp.minimum(z // 4, 1))
         def _():
             forward_anchor()
 
         need(2 * p)
         need(2 * p + 1)
-
-        @pl.when(me > 0)
+        bare = (p == 0) & (y == 0)
+
+        @pl.when(bare & (me > 0))
+        def _():
+            compute([1])
+
+        @pl.when(jnp.logical_not(bare))
         def _():
             compute([2 * p, 2 * p + 1])
 
-    loop(0, (z + 2) // 2, pair)
-
-    @pl.when(z % 2 == 1)
-    def _():
-        need(z + 1)
-        compute([z + 1])
+    odd = z % 2
+    loop(0, (z + 2 - 3 * odd) // 2, pair)
+
+    @pl.when(z == 1)
+    def _():
+        forward(0)
+        forward_anchor()
+
+    @pl.when(odd == 1)
+    def _():
+        tiles = [z - 1, z, z + 1]
+        for t in tiles:
+            need(t)
+        compute(tiles)
 
     for c in range(blk // TILE):
         for h in range(heads):
@@ -249,10 +310,16 @@
                 acc[r, :HEAD_DIM] / acc[r, HEAD_DIM:]).astype(BF16)
 
     def gone(i):
-        for d in range(1, RING):
+        @pl.when(i >= NEAR)
+        def _():
+            across(i, 2).wait_send()
+
+        for d in (1, 3):
             across(i, d).wait_send()
 
     loop(0, z, gone)
+    swap.wait_send()
+    loop(0, near, lambda i: down_far(i).wait_send())
     for d in range(1, RING):
         across_anchor(d).wait_send()
     loop(y + 1, RING, lambda c: to_row(c).wait_send())
@@ -290,11 +357,13 @@
             pltpu.VMEM((ANCHOR_TOKENS, 2 * HEAD_DIM), BF16),
             pltpu.VMEM(((rows + 1) * TILE, HEAD_DIM), BF16),
             pltpu.VMEM((ret, 2 * HEAD_DIM), BF16),
+            pltpu.VMEM((ret, 2 * HEAD_DIM), BF16),
             pltpu.VMEM((blk * heads, 2 * HEAD_DIM), F32),
             pltpu.VMEM((blk * heads, HEAD_DIM), F32),
             dma((4,)),
+            pltpu.SemaphoreType.REGULAR,
             dma((rows,)), dma((rows,)), dma((RING, rows)), dma((RING, rows)),
-            dma((RING,)), dma((RING,)), dma((RING,)),
+            dma((RING,)), dma((RING,)), dma((2,)), dma((NEAR,)), dma((RING,)),
             dma((1,)), dma((rows,)), dma((RING,)), dma((RING,)),
         ],
         compiler_params=pltpu.CompilerParams(

time: 29.7 us -> 28.1 us (0.946)
  the two profiles are of different devices: /device:TPU:102 before, /device:TPU:226 now
where the time goes in v4:
time: 28.1 us; the launch traced here: 27.9 us
  Pallas kernels  26.9 us (96%)
  local copies, waits for them, and re-layouts  0.97 us (3%)
    pallas_call x1, Pallas kernels, on_device(): pl.pallas_call(functools.partial(kernel, rows, heads), out_shape=pltpu.VM...  26.9 us
    unnamed x1, local copies, waits for them, and re-layouts  0.97 us

profile of v4, /device:TPU:226, one launch (start us, length us, event | category | flops | bytes accessed | tf_op | source)
XLA Modules:
  0.0 27.9 jit_solution(11836561021114219480)
XLA Ops:
  0.0 26.9 %shard_map.46 = bf16[512,1024]{1,0:T(8,128)(2,1)S(1)} custom-call(bf16[512,1024]{1,0:T(8,128)(2,1)} %q_hbm.1, bf16[512,128]{1,0:T(8,128)(2,1)} %k_hbm.1, bf16[512,128]{1,0:T(8,128)(2,1)} %v_hbm.1, s32[1,64]{1,0:T(1,128)} %bitcast.1), custom_call_target="tpu_custom_call" | custom-call | tf_op jit(solution)/shard_map/pallas_call | solution.py:345
  26.9 1.0 %copy.6 = bf16[512,1024]{1,0:T(8,128)(2,1)} copy(bf16[512,1024]{1,0:T(8,128)(2,1)S(1)} %shard_map.46) | data formatting | bytes 2097152

commit v5 on v4

--- a/solution.py
+++ b/solution.py
@@ -11,7 +11,7 @@
 ANCHOR_TOKENS = 256
 TILE = 256
 AHEAD = 4
-NEAR = 2
+NEAR = 1
 RING = 4
 LOG2_SCALE = HEAD_DIM**-0.5 * 1.4426950408889634
 NEG = -1e30
@@ -132,12 +132,10 @@
                 state = fold(state, s, v_buf[t * TILE:(t + 1) * TILE, :], jnp.ones((TILE, HEAD_DIM), BF16))
             top[r, :], acc[r, :] = state
 
-    def compute(tiles):
-        state = top[...], acc[...]
-        for t in tiles:
-            r = pl.ds(pl.multiple_of(t * TILE, TILE), TILE)
-            state = fold(state, scores_of(q2_buf[...], kv[r, :HEAD_DIM]), kv[r, HEAD_DIM:], ones[r, :])
-        top[...], acc[...] = state
+    def compute(t):
+        r = pl.ds(pl.multiple_of(t * TILE, TILE), TILE)
+        s = scores_of(q2_buf[...], kv[r, :HEAD_DIM])
+        top[...], acc[...] = fold((top[...], acc[...]), s, kv[r, HEAD_DIM:], ones[r, :])
 
     swap = remote(mine, other, s_sem.at[0], s_sem.at[1], at(z, (y + 2) % RING))
 
@@ -214,7 +212,12 @@
         pl.semaphore_signal(ready, inc=1, device_id=at(0, y), device_id_type=MESH)
 
     swap.start()
-    loop(0, last - z, lambda i: down(last - i).start())
+    mid = rows // 2
+    for t in [last, mid - 1] + [t for t in range(last - 1, 0, -1) if t != mid - 1]:
+        @pl.when(z < t)
+        def _():
+            down(t).start()
+
 
     @pl.when(z == 0)
     def _():
@@ -269,39 +272,27 @@
             for d in range(1, RING):
                 from_across_anchor(d).wait_recv()
 
-    def pair(p):
-        loop(jnp.minimum(z, AHEAD * p), jnp.minimum(z, AHEAD * (p + 1)), forward)
-
-        @pl.when(p == jnp.minimum(z // 4, 1))
+    low = z // (rows // 2)
+
+    def step(k):
+        late = (k + rows - z) // rows
+        tile = k + low * late * (1 - 2 * (k - z))
+
+        @pl.when(k > 0)
+        def _():
+            loop(jnp.minimum(z, AHEAD * (k - 1)), jnp.minimum(z, AHEAD * k), forward)
+
+        @pl.when(k == 1 + 2 * low)
         def _():
             forward_anchor()
 
-        need(2 * p)
-        need(2 * p + 1)
-        bare = (p == 0) & (y == 0)
-
-        @pl.when(bare & (me > 0))
-        def _():
-            compute([1])
-
-        @pl.when(jnp.logical_not(bare))
-        def _():
-            compute([2 * p, 2 * p + 1])
-
-    odd = z % 2
-    loop(0, (z + 2 - 3 * odd) // 2, pair)
-
-    @pl.when(z == 1)
-    def _():
-        forward(0)
-        forward_anchor()
-
-    @pl.when(odd == 1)
-    def _():
-        tiles = [z - 1, z, z + 1]
-        for t in tiles:
-            need(t)
-        compute(tiles)
+        need(tile)
+
+        @pl.when((me > 0) & (k + y > 0))
+        def _():
+            compute(tile)
+
+    loop(0, z + 2, step)
 
     for c in range(blk // TILE):
         for h in range(heads):

time: 28.1 us -> 27.8 us (0.989)
  Pallas kernels: 26.9 us -> 26.6 us
    pallas_call x1, Pallas kernels: 26.9 us -> 26.6 us  [on_device(): pl.pallas_call(functools.partial(kernel, rows, heads), out_shape=pltpu.VM...]
where the time goes in v5:
time: 27.8 us; the launch traced here: 27.6 us
  Pallas kernels  26.6 us (96%)
  local copies, waits for them, and re-layouts  0.97 us (3%)
    pallas_call x1, Pallas kernels, on_device(): pl.pallas_call(functools.partial(kernel, rows, heads), out_shape=pltpu.VM...  26.6 us
    unnamed x1, local copies, waits for them, and re-layouts  0.97 us

profile of v5, /device:TPU:226, one launch (start us, length us, event | category | flops | bytes accessed | tf_op | source)
XLA Modules:
  0.0 27.6 jit_solution(11052190700402849173)
XLA Ops:
  0.0 26.6 %shard_map.46 = bf16[512,1024]{1,0:T(8,128)(2,1)S(1)} custom-call(bf16[512,1024]{1,0:T(8,128)(2,1)} %q_hbm.1, bf16[512,128]{1,0:T(8,128)(2,1)} %k_hbm.1, bf16[512,128]{1,0:T(8,128)(2,1)} %v_hbm.1, s32[1,64]{1,0:T(1,128)} %bitcast.1), custom_call_target="tpu_custom_call" | custom-call | tf_op jit(solution)/shard_map/pallas_call | solution.py:336
  26.6 1.0 %copy.6 = bf16[512,1024]{1,0:T(8,128)(2,1)} copy(bf16[512,1024]{1,0:T(8,128)(2,1)S(1)} %shard_map.46) | data formatting | bytes 2097152

commit v6 on v5

--- a/solution.py
+++ b/solution.py
@@ -11,7 +11,7 @@
 ANCHOR_TOKENS = 256
 TILE = 256
 AHEAD = 4
-NEAR = 1
+NEAR = 2
 RING = 4
 LOG2_SCALE = HEAD_DIM**-0.5 * 1.4426950408889634
 NEG = -1e30
@@ -132,10 +132,20 @@
                 state = fold(state, s, v_buf[t * TILE:(t + 1) * TILE, :], jnp.ones((TILE, HEAD_DIM), BF16))
             top[r, :], acc[r, :] = state
 
-    def compute(t):
+    def folded(t):
         r = pl.ds(pl.multiple_of(t * TILE, TILE), TILE)
         s = scores_of(q2_buf[...], kv[r, :HEAD_DIM])
-        top[...], acc[...] = fold((top[...], acc[...]), s, kv[r, HEAD_DIM:], ones[r, :])
+        return fold((top[...], acc[...]), s, kv[r, HEAD_DIM:], ones[r, :])
+
+    def compute(t):
+        top[...], acc[...] = folded(t)
+
+    def finish(total):
+        for c in range(blk // TILE):
+            for h in range(heads):
+                r = slice(c * both + h * TILE, c * both + (h + 1) * TILE)
+                o_ref[c * TILE:(c + 1) * TILE, h * HEAD_DIM:(h + 1) * HEAD_DIM] = (
+                    total[r, :HEAD_DIM] / total[r, HEAD_DIM:]).astype(BF16)
 
     swap = remote(mine, other, s_sem.at[0], s_sem.at[1], at(z, (y + 2) % RING))
 
@@ -212,12 +222,7 @@
         pl.semaphore_signal(ready, inc=1, device_id=at(0, y), device_id_type=MESH)
 
     swap.start()
-    mid = rows // 2
-    for t in [last, mid - 1] + [t for t in range(last - 1, 0, -1) if t != mid - 1]:
-        @pl.when(z < t)
-        def _():
-            down(t).start()
-
+    loop(0, last - z, lambda i: down(last - i).start())
 
     @pl.when(z == 0)
     def _():
@@ -230,13 +235,24 @@
         own_block()
 
     swap.wait_recv()
-    near = jnp.minimum(NEAR, last - z)
-    loop(0, near, lambda i: down_far(i).start())
+    doubled = 1 + (NEAR - 1) * (z // last)
+
+    def each_far(go):
+        @pl.when(z < last)
+        def _():
+            go(down_far(0))
+
+        for i in range(1, NEAR):
+            @pl.when(z + 1 + i == last)
+            def _():
+                go(down_far(i))
+
+    each_far(lambda copy: copy.start())
 
     def forward(i):
         from_above(i).wait_recv()
 
-        @pl.when(i >= NEAR)
+        @pl.when(i >= doubled)
         def _():
             across(i, 2).start()
 
@@ -287,21 +303,28 @@
             forward_anchor()
 
         need(tile)
+        return tile
+
+    def work(k):
+        tile = step(k)
 
         @pl.when((me > 0) & (k + y > 0))
         def _():
             compute(tile)
 
-    loop(0, z + 2, step)
-
-    for c in range(blk // TILE):
-        for h in range(heads):
-            r = slice(c * both + h * TILE, c * both + (h + 1) * TILE)
-            o_ref[c * TILE:(c + 1) * TILE, h * HEAD_DIM:(h + 1) * HEAD_DIM] = (
-                acc[r, :HEAD_DIM] / acc[r, HEAD_DIM:]).astype(BF16)
+    loop(0, z + 1, work)
+    final = step(z + 1)
+
+    @pl.when(me > 0)
+    def _():
+        finish(folded(final)[1])
+
+    @pl.when(me == 0)
+    def _():
+        finish(acc[...])
 
     def gone(i):
-        @pl.when(i >= NEAR)
+        @pl.when(i >= doubled)
         def _():
             across(i, 2).wait_send()
 
@@ -310,7 +333,7 @@
 
     loop(0, z, gone)
     swap.wait_send()
-    loop(0, near, lambda i: down_far(i).wait_send())
+    each_far(lambda copy: copy.wait_send())
     for d in range(1, RING):
         across_anchor(d).wait_send()
     loop(y + 1, RING, lambda c: to_row(c).wait_send())

time: 27.8 us -> 27 us (0.971)
  Pallas kernels: 26.6 us -> 25.9 us
    pallas_call x1, Pallas kernels: 26.6 us -> 25.9 us  [on_device(): pl.pallas_call(functools.partial(kernel, rows, heads), out_shape=pltpu.VM...]
where the time goes in v6:
time: 27 us; the launch traced here: 26.9 us
  Pallas kernels  25.9 us (96%)
  local copies, waits for them, and re-layouts  0.97 us (4%)
    pallas_call x1, Pallas kernels, on_device(): pl.pallas_call(functools.partial(kernel, rows, heads), out_shape=pltpu.VM...  25.9 us
    unnamed x1, local copies, waits for them, and re-layouts  0.97 us

profile of v6, /device:TPU:226, one launch (start us, length us, event | category | flops | bytes accessed | tf_op | source)
XLA Modules:
  0.0 26.9 jit_solution(13274251360557154016)
XLA Ops:
  0.0 25.9 %shard_map.46 = bf16[512,1024]{1,0:T(8,128)(2,1)S(1)} custom-call(bf16[512,1024]{1,0:T(8,128)(2,1)} %q_hbm.1, bf16[512,128]{1,0:T(8,128)(2,1)} %k_hbm.1, bf16[512,128]{1,0:T(8,128)(2,1)} %v_hbm.1, s32[1,64]{1,0:T(1,128)} %bitcast.1), custom_call_target="tpu_custom_call" | custom-call | tf_op jit(solution)/shard_map/pallas_call | solution.py:359
  26.0 1.0 %copy.6 = bf16[512,1024]{1,0:T(8,128)(2,1)} copy(bf16[512,1024]{1,0:T(8,128)(2,1)S(1)} %shard_map.46) | data formatting | bytes 2097152

commit v7 on v6

--- a/solution.py
+++ b/solution.py
@@ -226,7 +226,8 @@
 
     @pl.when(z == 0)
     def _():
-        loop(0, last, lambda i: down_anchor(last - i).start())
+        down_anchor(last).start()
+        loop(1, last, lambda t: down_anchor(t).start())
 
     loop(y + 1, RING, lambda c: to_row(c).start())
 

time: 27 us -> 27 us (level)
  no operation moved by 1% of the time
where the time goes in v7:
time: 27 us; the launch traced here: 26.9 us
  Pallas kernels  25.9 us (96%)
  local copies, waits for them, and re-layouts  0.97 us (4%)
    pallas_call x1, Pallas kernels, on_device(): pl.pallas_call(functools.partial(kernel, rows, heads), out_shape=pltpu.VM...  25.9 us
    unnamed x1, local copies, waits for them, and re-layouts  0.97 us

profile of v7, /device:TPU:226, one launch (start us, length us, event | category | flops | bytes accessed | tf_op | source)
XLA Modules:
  0.0 26.9 jit_solution(7591286481030888826)
XLA Ops:
  0.0 25.9 %shard_map.46 = bf16[512,1024]{1,0:T(8,128)(2,1)S(1)} custom-call(bf16[512,1024]{1,0:T(8,128)(2,1)} %q_hbm.1, bf16[512,128]{1,0:T(8,128)(2,1)} %k_hbm.1, bf16[512,128]{1,0:T(8,128)(2,1)} %v_hbm.1, s32[1,64]{1,0:T(1,128)} %bitcast.1), custom_call_target="tpu_custom_call" | custom-call | tf_op jit(solution)/shard_map/pallas_call | solution.py:360
  26.0 1.0 %copy.6 = bf16[512,1024]{1,0:T(8,128)(2,1)} copy(bf16[512,1024]{1,0:T(8,128)(2,1)S(1)} %shard_map.46) | data formatting | bytes 2097152
